TPU v7x, 512 devices: a whole 4x8x8 slice. The times are simulated.
512 devices in a mesh: row: 16 (over y_hi, x, core), col: 32 (over y_lo, z).
Axes of the slice: x: 4, y: 8 (y_hi: 2, y_lo: 4; y = y_hi * 4 + y_lo), z: 8, core: 2. Of those that a mesh axis runs over, the one named last changes fastest.
Arguments:
- tokens_fwd: bfloat16 [512, 12288], P('col', 'row'), may hold values from -6 to 6
- tokens_bwd: bfloat16 [512, 12288], P('col', 'row'), may hold values from -6 to 6
- weight: bfloat16 [12288, 24576], P('row', 'col'), may hold values from -0.0546875 to 0.0546875
- bias: float32 [24576], P('col'), may hold values from -3 to 3
- preact: bfloat16 [512, 24576], P('row', 'col'), may hold values from -8 to 8
- upstream: bfloat16 [512, 24576], P('row', 'col'), may hold values from -3 to 3
Outputs:
- hidden: bfloat16 [512, 24576], P('row', 'col')
- input_grad: bfloat16 [512, 12288], P('col', 'row')
- weight_grad: float32 [12288, 24576], P('row', 'col')
- bias_grad: float32 [24576], P('col')
All inputs are finite; a program needn't handle non-finite values.
Results may differ from a plain program's by a relative error of at most 0.0049.
Values may be sent and summed in bfloat16 or wider, within the bound.
A program may use at most 64 MiB of HBM per device.

v0:
```python
import math

import jax
import jax.numpy as jnp
from jax import lax
from jax.sharding import PartitionSpec as P

gelu_scale = math.sqrt(2.0 / math.pi)
cubic_term = 0.044715


def gelu_tanh(values):
    inner_arg = gelu_scale * (values + cubic_term * values * values * values)
    return 0.5 * values * (1.0 + jnp.tanh(inner_arg))


def gelu_slope(values):
    tangent = jnp.tanh(gelu_scale * (values + cubic_term * values * values * values))
    return 0.5 * (1.0 + tangent) + 0.5 * values * (1.0 - tangent * tangent) * gelu_scale * (
        1.0 + 3.0 * cubic_term * values * values
    )


def local(tokens_fwd, tokens_bwd, weight, bias, preact, upstream):
    full_fwd, full_bwd = (
        lax.all_gather(tokens_fwd, "col", axis=0, tiled=True),
        lax.all_gather(tokens_bwd, "col", axis=0, tiled=True),
    )
    piece = full_fwd
    reduced = lax.psum_scatter(
        jnp.dot(piece, weight, preferred_element_type=jnp.float32),
        "row",
        scatter_dimension=0,
        tiled=True,
    )
    hidden = gelu_tanh(reduced + bias).astype(jnp.bfloat16)
    local_grad = (upstream.astype(jnp.float32) * gelu_slope(preact.astype(jnp.float32))).astype(
        jnp.bfloat16
    )
    gathered = lax.all_gather(local_grad, "row", axis=0, tiled=True)
    piece = gathered
    input_grad = lax.psum_scatter(
        lax.dot_general(
            piece, weight, (((1,), (1,)), ((), ())), preferred_element_type=jnp.float32
        ),
        "col",
        scatter_dimension=0,
        tiled=True,
    ).astype(jnp.bfloat16)
    weight_grad = lax.dot_general(
        full_bwd, gathered, (((0,), (0,)), ((), ())), preferred_element_type=jnp.float32
    )
    row_count = gathered.shape[0] // lax.axis_size("row")
    own_grad = lax.dynamic_slice_in_dim(gathered, lax.axis_index("row") * row_count, row_count, 0)
    bias_grad = lax.psum(jnp.sum(own_grad.astype(jnp.float32), axis=0), "row")
    input_grad, weight_grad, bias_grad = (input_grad, weight_grad, bias_grad)
    return (hidden, input_grad, weight_grad, bias_grad)


def solution(mesh):
    return jax.shard_map(
        local,
        mesh=mesh,
        in_specs=(
            P("col", "row"),
            P("col", "row"),
            P("row", "col"),
            P("col"),
            P("row", "col"),
            P("row", "col"),
        ),
        out_specs=(P("row", "col"), P("col", "row"), P("row", "col"), P("col")),
        check_vma=False,
    )
```

profile of v0, /device:TPU:6, one launch (start us, length us, event | category | flops | bytes accessed | tf_op | source)
XLA Modules:
  0.0 354.6 jit_solution(8092951345516969000)
XLA Ops:
  7.2 0.0 copy-start
  7.2 0.0 reduce-scatter.3.cloned.1.call-start
  7.2 89.5 %all_gather.9 = bf16[512,768]{1,0:T(8,128)(2,1)S(1)} all-gather(bf16[16,768]{1,0:T(8,128)(2,1)} %param.6), channel_id=1, replica_groups=mesh['row'=16,'col'=32] {'col'}, dimensions={0}, use_global_device_ids=true | all-gather | bytes 811008 | tf_op jit(solution)/shard_map/all_gather | solution.py:26
  96.7 0.0 copy-done
  96.7 1.9 fusion.14
  98.7 0.0 copy-start.2
  98.7 0.0 copy-start.3
  98.7 0.0 reduce-scatter.3.cloned.1.call-update
  98.7 0.0 reduce-scatter.5.cloned.1.call-start
  98.7 0.7 copy-done.2
  99.5 0.0 copy-done.3
  99.5 0.1 fusion.12
  99.6 25.0 %all_gather.10 = bf16[512,768]{1,0:T(8,128)(2,1)S(1)} all-gather(bf16[32,768]{1,0:T(8,128)(2,1)S(1)} %fusion.12), channel_id=1, replica_groups=mesh['row'=16,'col'=32] {'row'}, dimensions={0}, use_global_device_ids=true | all-gather | bytes 835584 | tf_op jit(solution)/shard_map/all_gather | solution.py:40
  124.5 0.0 copy-start.1
  124.5 0.9 copy-done.1
  125.4 2.0 fusion.15
  127.4 0.0 copy-start.4
  127.4 0.0 reduce-scatter.5.cloned.1.call-update
  127.4 0.7 copy-done.4
  128.1 79.7 %all_gather.11 = bf16[512,768]{1,0:T(8,128)(2,1)S(1)} all-gather(bf16[16,768]{1,0:T(8,128)(2,1)S(1)} %copy-done.4), channel_id=1, replica_groups=mesh['row'=16,'col'=32] {'col'}, dimensions={0}, use_global_device_ids=true | all-gather | bytes 811008 | tf_op jit(solution)/shard_map/all_gather | solution.py:27
  207.8 1.9 convolution_bitcast_fusion
  209.8 0.0 copy-start.5
  209.8 2.0 copy.10
  211.7 0.8 convert_reduce_fusion
  212.5 44.5 %psum.7 = f32[768]{0:T(1024)} all-reduce(f32[768]{0:T(1024)S(1)} %convert_reduce_fusion), channel_id=1, replica_groups=mesh['row'=16,'col'=32] {'row'}, use_global_device_ids=true, to_apply=%region_3.0 | all-reduce | flops 768 | bytes 6144 | tf_op jit(solution)/shard_map/psum | solution.py:55
  257.0 0.0 reduce-scatter.3.cloned.1.call-done
  257.0 0.0 copy-done.5
  257.0 1.6 fusion.4
  258.6 87.8 %reduce-scatter.5.cloned.1.call-done = f32[16,768]{1,0:T(8,128)} async-done(((f32[512,768]{1,0:T(8,128)}), f32[16,768]{1,0:T(8,128)}) %reduce-scatter.5.cloned.1.call-update) | async-done | bytes 49168 | tf_op jit(solution)/shard_map/reduce_scatter | solution.py:42
  346.4 1.4 convert_element_type.22
Async XLA Ops:
  7.2 89.6 %copy-start = (bf16[768,768]{1,0:T(8,128)(2,1)S(1)}, bf16[768,768]{1,0:T(8,128)(2,1)}, u32[]{:S(2)}) copy-start(bf16[768,768]{1,0:T(8,128)(2,1)} %param.8) | copy-start | bytes 3538948
  7.2 249.8 %reduce-scatter.3.cloned.1.call-start = ((), (), s32[]{:S(2)}) async-start(), calls=%async_computation.2 | async-start | bytes 1671168 | tf_op jit(solution)/shard_map/reduce_scatter | solution.py:30
  98.7 0.8 copy-start.2
  98.7 0.8 copy-start.3
  98.7 247.7 %reduce-scatter.5.cloned.1.call-start = ((), (), s32[]{:S(2)}) async-start(), calls=%async_computation.3 | async-start | bytes 1622016 | tf_op jit(solution)/shard_map/reduce_scatter | solution.py:42
  124.5 0.9 copy-start.1
  127.4 0.7 copy-start.4
  209.8 47.3 %copy-start.5 = (f32[768]{0:T(1024)S(1)}, f32[768]{0:T(1024)}, u32[]{:S(2)}) copy-start(f32[768]{0:T(1024)} %param.9) | copy-start | bytes 9220
Sparse Core Ops, SparseCore 0:
  98.8 84.8 reduce-scatter.2
  186.5 159.8 reduce-scatter.4
where the time goes:
time: 355 us
  blocking collectives  239 us (67%)
  waiting for transfers between devices  87.9 us (25%)
  between operations  14.1 us (4%)
  matrix products  5.84 us (2%)
  local copies, waits for them, and re-layouts  4.3 us (1%)
  other arithmetic  3.86 us (1%)
    all_gather x1, blocking collectives, local(): lax.all_gather(tokens_fwd, 'col', axis=0, tiled=True)  89.5 us
    reduce_scatter x1, waiting for transfers between devices, local(): lax.psum_scatter(lax.dot_general(piece, weight, (((1,), (1,)), ((), ())),...  87.8 us
    all_gather x1, blocking collectives, local(): lax.all_gather(tokens_bwd, 'col', axis=0, tiled=True)  79.7 us
    psum x1, blocking collectives, local(): bias_grad = lax.psum(jnp.sum(own_grad.astype(jnp.float32), axis=0), 'row')  44.5 us
    all_gather x1, blocking collectives, local(): gathered = lax.all_gather(local_grad, 'row', axis=0, tiled=True)  25 us
  transfers between devices with their start and end apart: 2, of which 1 were waited for; matrix products, arithmetic and copies ran while one was open for 2% of the time, Pallas kernels for 0%

commit v1 on v0

v1 whole, which is shorter than its diff:
```python
import math

import jax
import jax.numpy as jnp
from jax import lax
from jax.experimental import pallas as pl
from jax.experimental.pallas import tpu as pltpu
from jax.sharding import PartitionSpec as P

gelu_scale = math.sqrt(2.0 / math.pi)
cubic_term = 0.044715
F32, BF16 = jnp.float32, jnp.bfloat16
MESH = pl.DeviceIdType.MESH
TILE = 256


def gelu_tanh(values):
    inner_arg = gelu_scale * (values + cubic_term * values * values * values)
    return 0.5 * values * (1.0 + jnp.tanh(inner_arg))


def gelu_slope(values):
    tangent = jnp.tanh(gelu_scale * (values + cubic_term * values * values * values))
    return 0.5 * (1.0 + tangent) + 0.5 * values * (1.0 - tangent * tangent) * gelu_scale * (
        1.0 + 3.0 * cubic_term * values * values
    )


def flip(i, k):
    if k == 1:
        return i + 1 - 2 * lax.rem(i, 2)
    if k == 2:
        return lax.rem(i + 2, 4)
    return 3 - i


class Sems:
    def __init__(self, send, recv):
        self.send, self.recv, self.n = send, recv, 0

    def pair(self):
        self.n += 1
        return self.send.at[self.n - 1], self.recv.at[self.n - 1]


N_LOCAL = 6
N_REMOTE = 80


def kernel(
    fwd_hbm, bwd_hbm, w_hbm, bias_hbm, pre_hbm, up_hbm,
    hidden_ref, igrad_ref, wgrad_ref, bgrad_ref,
    xf, xb, g, q, w, bias, pre, up,
    half, core_out, core_in, x_out, x_in, y_out, y_in,
    rs_out, rs_in, line_out, line_in, sums,
    local_sem, send_sem, recv_sem,
):
    row, col = lax.axis_index("row"), lax.axis_index("col")
    yh, x, core = row // 8, lax.rem(row // 2, 4), lax.rem(row, 2)
    yl, z = col // 8, lax.rem(col, 8)
    early = yl // 2

    def device(yh=yh, x=x, core=core, yl=yl, z=z):
        return (yh * 8 + x * 2 + core, yl * 8 + z)

    up_z, down_z = lax.rem(z + 1, 8), lax.rem(z + 7, 8)
    near_z = (device(z=up_z), device(z=down_z))
    near_x = [device(x=flip(x, k)) for k in (1, 2, 3)]
    near_y = [device(yl=flip(yl, k)) for k in (1, 2, 3)]
    far_y = device(yh=1 - yh)
    twin = device(core=1 - core)
    partners = [*near_z, *near_x, *near_y, far_y, twin]

    sems = Sems(send_sem, recv_sem)
    started = []

    def copy(src, dst, target):
        s, r = sems.pair()
        c = pltpu.make_async_remote_copy(
            src_ref=src, dst_ref=dst, send_sem=s, recv_sem=r,
            device_id=target, device_id_type=MESH,
        )
        started.append(c)
        return c

    def at_z(ref, pair, at):
        return ref.at[pl.ds(2 * pair, 2), at // 4, lax.rem(at // 2, 2), lax.rem(at, 2)]

    def own(ref):
        return ref.at[yl, z // 4, lax.rem(z // 2, 2), lax.rem(z, 2)]

    def from_y(ref, at):
        return ref.at[at, z // 4, lax.rem(z // 2, 2), lax.rem(z, 2)]

    loads = [
        pltpu.make_async_copy(src, dst, local_sem.at[i])
        for i, (src, dst) in enumerate(
            [(fwd_hbm, own(xf)), (pre_hbm, pre), (up_hbm, up), (bwd_hbm, own(xb)), (w_hbm, w), (bias_hbm, bias)]
        )
    ]
    for c in loads:
        c.start()
    barrier = pltpu.get_barrier_semaphore()
    for d in partners:
        pl.semaphore_signal(barrier, inc=1, device_id=d, device_id_type=MESH)
    for c in loads[:4]:
        c.wait()
    grad = (up[...].astype(F32) * gelu_slope(pre[...].astype(F32))).astype(BF16)
    g[yh, x, core] = grad
    pl.semaphore_wait(barrier, len(partners))

    def line(ref):
        return [copy(own(ref), own(ref), near_y[k - 1]) for k in (1, 2, 3)]

    f_line = line(xf)
    for c in f_line:
        c.start()
    g_far = copy(g.at[yh, x, core], g.at[yh, x, core], far_y)
    g_far.start()
    g_x = [copy(g.at[yh, x, core], g.at[yh, x, core], d) for d in near_x]
    for c in g_x:
        c.start()
    b_line = line(xb)
    for c in b_line:
        c.start()

    class Ring:
        def __init__(self, ref):
            self.ref = ref
            self.pairs = (early, 1 - early)
            self.hops = ((4, 3), (3, 4))
            self.sent = {}

        def step(self, s, which):
            for way in (0, 1):
                if s >= self.hops[which][way]:
                    continue
                if s > 0:
                    self.sent[s - 1, which, way].wait_recv()
                source = lax.rem(z - s + 8, 8) if way == 0 else lax.rem(z + s, 8)
                block = at_z(self.ref, self.pairs[which], source)
                c = copy(block, block, near_z[way])
                c.start()
                self.sent[s, which, way] = c

        def finish(self):
            for which in (0, 1):
                for way in (0, 1):
                    self.sent[self.hops[which][way] - 1, which, way].wait_recv()

    f_ring, b_ring = Ring(xf), Ring(xb)
    f_line[0].wait_recv()
    f_ring.step(0, 0)
    f_line[1].wait_recv()
    f_line[2].wait_recv()
    f_ring.step(0, 1)
    f_ring.step(1, 0)
    f_ring.step(1, 1)
    for c in g_x:
        c.wait_recv()
    g_twin = [copy(g.at[yh, :, core], g.at[yh, :, core], twin)]
    g_twin[0].start()
    g_far.wait_recv()
    g_x2 = [copy(g.at[1 - yh, x, core], g.at[1 - yh, x, core], d) for d in near_x]
    for c in g_x2:
        c.start()
    f_ring.step(2, 0)
    f_ring.step(2, 1)
    f_ring.step(3, 0)
    f_ring.step(3, 1)
    for c in b_line:
        c.wait_recv()
    b_ring.step(0, 0)
    b_ring.step(0, 1)
    for c in g_x2:
        c.wait_recv()
    g_twin.append(copy(g.at[1 - yh, :, core], g.at[1 - yh, :, core], twin))
    g_twin[1].start()
    loads[4].wait()
    loads[5].wait()

    f_ring.finish()

    def forward_half(which, store):
        lhs = xf[:, :, which].reshape(256, 768)

        def body(n, carry):
            at = pl.ds(pl.multiple_of(n * TILE, TILE), TILE)
            store(at, jnp.dot(lhs, w[:, at], preferred_element_type=F32).reshape(2, 4, 32, TILE))
            return carry

        lax.fori_loop(0, 3, body, 0)

    def store_out(at, value):
        core_out[:, :, :, at] = value.astype(BF16)

    def store_half(at, value):
        half[:, :, :, at] = value

    forward_half(1 - core, store_out)
    c_twin = copy(core_out, core_in, twin)
    c_twin.start()

    for c in g_twin:
        c.wait_recv()

    def q_body(n, carry):
        at = pl.ds(pl.multiple_of(n * TILE, TILE), TILE)
        q[:, :, :, at] = lax.dot_general(
            g[...].reshape(512, 768), w[at, :], (((1,), (1,)), ((), ())), preferred_element_type=F32
        ).reshape(4, 8, 16, TILE)
        return carry

    lax.fori_loop(0, 3, q_body, 0)

    rs_hops = ((4, 3), (3, 4))
    rs_sent = {}
    slot_of = {}
    for pair in (0, 1):
        for way in (0, 1):
            for s in range(rs_hops[pair][way]):
                slot_of[s, pair, way] = len(slot_of)

    def rs_step(s, pair):
        for way in (0, 1):
            hops = rs_hops[pair][way]
            if s >= hops:
                continue
            left = hops - s
            target = lax.rem(z + left, 8) if way == 0 else lax.rem(z - left + 8, 8)
            value = q[pl.ds(2 * pair, 2), target]
            if s > 0:
                before = rs_sent[s - 1, pair, way]
                before.wait_recv()
                value = value + rs_in[slot_of[s - 1, pair, way]].astype(F32)
            slot = slot_of[s, pair, way]
            rs_out[slot] = value.astype(BF16)
            c = copy(rs_out.at[slot], rs_in.at[slot], near_z[way])
            c.start()
            rs_sent[s, pair, way] = c

    rs_step(0, 0)
    rs_step(0, 1)
    forward_half(core, store_half)
    b_ring.step(1, 0)
    b_ring.step(1, 1)
    c_twin.wait_recv()
    half[...] = half[...] + core_in[...].astype(F32)
    x_copies = []
    for k in (1, 2, 3):
        x_out[k - 1] = half[:, flip(x, k)].astype(BF16)
        c = copy(x_out.at[k - 1], x_in.at[k - 1], near_x[k - 1])
        c.start()
        x_copies.append(c)
    rs_step(1, 0)
    rs_step(1, 1)
    bgrad_ref[...] = jnp.sum(g[...].reshape(512, 768).astype(F32), axis=0, keepdims=True)
    b_ring.step(2, 0)
    b_ring.step(2, 1)
    rs_step(2, 0)
    rs_step(2, 1)
    for c in x_copies:
        c.wait_recv()
    sums[...] = half[:, x] + x_in[0].astype(F32) + x_in[1].astype(F32) + x_in[2].astype(F32)
    y_out[...] = sums[1 - yh].astype(BF16)
    c_far = copy(y_out, y_in, far_y)
    c_far.start()
    b_ring.step(3, 0)
    b_ring.step(3, 1)
    rs_step(3, 0)
    rs_step(3, 1)

    for pair in (0, 1):
        value = q[pl.ds(2 * pair, 2), z]
        for way in (0, 1):
            s = rs_hops[pair][way] - 1
            rs_sent[s, pair, way].wait_recv()
            value = value + rs_in[slot_of[s, pair, way]].astype(F32)
        q[pl.ds(2 * pair, 2), z] = value
    l_copies = []
    for k in (1, 2, 3):
        line_out[k - 1] = q[flip(yl, k), z].astype(BF16)
        c = copy(line_out.at[k - 1], line_in.at[k - 1], near_y[k - 1])
        c.start()
        l_copies.append(c)

    c_far.wait_recv()
    hidden_ref[...] = gelu_tanh(sums[yh] + y_in[...].astype(F32) + bias[...]).astype(BF16)

    b_ring.finish()

    def w_body(n, carry):
        at = pl.ds(pl.multiple_of(n * TILE, TILE), TILE)
        wgrad_ref[at, :] = lax.dot_general(
            xb[:, :, :, :, :, at].reshape(512, TILE), g[...].reshape(512, 768), (((0,), (0,)), ((), ())),
            preferred_element_type=F32,
        )
        return carry

    lax.fori_loop(0, 3, w_body, 0)

    for c in l_copies:
        c.wait_recv()
    igrad_ref[...] = (
        q[yl, z] + line_in[0].astype(F32) + line_in[1].astype(F32) + line_in[2].astype(F32)
    ).astype(BF16)
    for c in started:
        c.wait_send()


def local(tokens_fwd, tokens_bwd, weight, bias, preact, upstream):
    any_space = pl.BlockSpec(memory_space=pl.ANY)
    vmem = pl.BlockSpec(memory_space=pltpu.VMEM)
    hidden, input_grad, weight_grad, bias_grad = pl.pallas_call(
        kernel,
        out_shape=(
            jax.ShapeDtypeStruct((32, 768), BF16),
            jax.ShapeDtypeStruct((16, 768), BF16),
            jax.ShapeDtypeStruct((768, 768), F32),
            jax.ShapeDtypeStruct((1, 768), F32),
        ),
        in_specs=[any_space] * 6,
        out_specs=[vmem] * 4,
        scratch_shapes=[
            pltpu.VMEM((4, 2, 2, 2, 16, 768), BF16),
            pltpu.VMEM((4, 2, 2, 2, 16, 768), BF16),
            pltpu.VMEM((2, 4, 2, 32, 768), BF16),
            pltpu.VMEM((4, 8, 16, 768), F32),
            pltpu.VMEM((768, 768), BF16),
            pltpu.VMEM((1, 768), F32),
            pltpu.VMEM((32, 768), BF16),
            pltpu.VMEM((32, 768), BF16),
            pltpu.VMEM((2, 4, 32, 768), F32),
            pltpu.VMEM((2, 4, 32, 768), BF16),
            pltpu.VMEM((2, 4, 32, 768), BF16),
            pltpu.VMEM((3, 2, 32, 768), BF16),
            pltpu.VMEM((3, 2, 32, 768), BF16),
            pltpu.VMEM((32, 768), BF16),
            pltpu.VMEM((32, 768), BF16),
            pltpu.VMEM((14, 2, 16, 768), BF16),
            pltpu.VMEM((14, 2, 16, 768), BF16),
            pltpu.VMEM((3, 16, 768), BF16),
            pltpu.VMEM((3, 16, 768), BF16),
            pltpu.VMEM((2, 32, 768), F32),
            pltpu.SemaphoreType.DMA((N_LOCAL,)),
            pltpu.SemaphoreType.DMA((N_REMOTE,)),
            pltpu.SemaphoreType.DMA((N_REMOTE,)),
        ],
        compiler_params=pltpu.CompilerParams(
            collective_id=0, has_side_effects=True, vmem_limit_bytes=48 * 2**20
        ),
        cost_estimate=pl.CostEstimate(flops=3 * 2 * 512 * 768 * 768, bytes_accessed=8 * 2**20, transcendentals=50000),
        name="feed_forward",
    )(tokens_fwd, tokens_bwd, weight, bias.reshape(1, 768), preact, upstream)
    return hidden, input_grad, weight_grad, bias_grad.reshape(768)


def solution(mesh):
    return jax.shard_map(
        local,
        mesh=mesh,
        in_specs=(
            P("col", "row"),
            P("col", "row"),
            P("row", "col"),
            P("col"),
            P("row", "col"),
            P("row", "col"),
        ),
        out_specs=(P("row", "col"), P("col", "row"), P("row", "col"), P("col")),
        check_vma=False,
    )
```

time: 355 us -> 66.7 us (0.19)
  blocking collectives: 239 us -> 0 us
  waiting for transfers between devices: 87.9 us -> 0 us
  Pallas kernels: 0 us -> 57.2 us
  between operations: 14.1 us -> 0.65 us
  matrix products: 5.84 us -> 0 us
    all_gather x3 -> x0, blocking collectives: 194 us -> none  [the longest x1 89.5 us: local(): lax.all_gather(tokens_fwd, 'col', axis=0, tiled=True)]
    reduce_scatter x2 -> x0, waiting for transfers between devices: 87.8 us -> none  [the longest x1 87.8 us: local(): lax.psum_scatter(lax.dot_general(piece, weight, (((1,), (1,)), ((), ())),...]
    pallas_call x0 -> x1, Pallas kernels: none -> 57.2 us  [local(): pl.pallas_call(kernel, out_shape=(jax.ShapeDtypeStruct((32, 768), BF16),...]
    psum x1 -> x0, blocking collectives: 44.5 us -> none  [local(): bias_grad = lax.psum(jnp.sum(own_grad.astype(jnp.float32), axis=0), 'row')]
    dot_general x3 -> x0, matrix products: 5.84 us -> none  [the longest x1 1.96 us: local(): lax.dot_general(piece, weight, (((1,), (1,)), ((), ())), preferred_elemen...]
  transfers between devices with their start and end apart: 2 -> 0, of which waited for: 1 -> 0; matrix products, arithmetic and copies ran while one was open for 2% -> 0% of each run, Pallas kernels for 0% -> 0%
where the time goes in v1:
time: 66.7 us; the launch traced here: 66.1 us
  Pallas kernels  57.2 us (86%)
  local copies, waits for them, and re-layouts  7.66 us (11%)
    pallas_call x1, Pallas kernels, local(): pl.pallas_call(kernel, out_shape=(jax.ShapeDtypeStruct((32, 768), BF16),...  57.2 us
    unnamed x13, local copies, waits for them, and re-layouts  6.97 us

profile of v1, /device:TPU:6, one launch (start us, length us, event | category | flops | bytes accessed | tf_op | source)
XLA Modules:
  0.0 66.1 jit_solution(12146246841507622615)
XLA Ops:
  0.6 0.7 %reshape.14.bias_hbm = f32[1,768]{1,0:T(1,128)S(1)} reshape(f32[768]{0:T(1024)} %param.9) | data formatting | bytes 6144 | tf_op jit(solution)/shard_map/reshape | solution.py:354
  1.3 0.0 copy-start
  1.3 1.3 %copy-done = bf16[768,768]{1,0:T(8,128)(2,1)S(1)} copy-done((bf16[768,768]{1,0:T(8,128)(2,1)S(1)}, bf16[768,768]{1,0:T(8,128)(2,1)}, u32[]{:S(2)}) %copy-start) | copy-done | bytes 1179672
  2.6 0.0 copy-start.1
  2.6 0.8 %copy-done.1 = bf16[32,768]{1,0:T(8,128)(2,1)S(1)} copy-done((bf16[32,768]{1,0:T(8,128)(2,1)S(1)}, bf16[32,768]{1,0:T(8,128)(2,1)}, u32[]{:S(2)}) %copy-start.1) | copy-done | bytes 49176
  3.4 0.0 copy-start.2
  3.4 0.8 %copy-done.2 = bf16[32,768]{1,0:T(8,128)(2,1)S(1)} copy-done((bf16[32,768]{1,0:T(8,128)(2,1)S(1)}, bf16[32,768]{1,0:T(8,128)(2,1)}, u32[]{:S(2)}) %copy-start.2) | copy-done | bytes 49176
  4.2 0.0 copy-start.3
  4.2 0.7 %copy-done.3 = bf16[16,768]{1,0:T(8,128)(2,1)S(1)} copy-done((bf16[16,768]{1,0:T(8,128)(2,1)S(1)}, bf16[16,768]{1,0:T(8,128)(2,1)}, u32[]{:S(2)}) %copy-start.3) | copy-done | bytes 24600
  4.9 0.0 copy-start.4
  4.9 0.7 %copy-done.4 = bf16[16,768]{1,0:T(8,128)(2,1)S(1)} copy-done((bf16[16,768]{1,0:T(8,128)(2,1)S(1)}, bf16[16,768]{1,0:T(8,128)(2,1)}, u32[]{:S(2)}) %copy-start.4) | copy-done | bytes 24600
  5.7 57.2 %feed_forward.1 = (bf16[32,768]{1,0:T(8,128)(2,1)S(1)}, bf16[16,768]{1,0:T(8,128)(2,1)S(1)}, f32[768,768]{1,0:T(8,128)S(1)}, f32[1,768]{1,0:T(1,128)S(1)}) custom-call(bf16[16,768]{1,0:T(8,128)(2,1)S(1)} %copy-done.3, bf16[16,768]{1,0:T(8,128)(2,1)S(1)} %copy-done.4, bf16[768,768]{1,0:T(8,128)(2,1)S(1)} %copy-done, f32[1,768]{1,0:T(1,128)S(1)} %reshape.14.bias_hbm, ...), custom_call_target="tpu_custom_call" | custom-call | flops 1811939328 | bytes 8388608 | tf_op jit(solution)/shard_map/feed_forward/pallas_call | solution.py:314
  62.9 0.6 reduce
  63.5 0.6 copy.13
  64.1 0.6 copy.14
  64.7 1.4 %copy.15 = f32[768,768]{1,0:T(8,128)} copy(f32[768,768]{1,0:T(8,128)S(1)} %get-tuple-element.18) | data formatting | bytes 4718592
Async XLA Ops:
  1.3 1.3 %copy-start = (bf16[768,768]{1,0:T(8,128)(2,1)S(1)}, bf16[768,768]{1,0:T(8,128)(2,1)}, u32[]{:S(2)}) copy-start(bf16[768,768]{1,0:T(8,128)(2,1)} %w_hbm.1) | copy-start | bytes 3538948
  2.6 0.8 %copy-start.1 = (bf16[32,768]{1,0:T(8,128)(2,1)S(1)}, bf16[32,768]{1,0:T(8,128)(2,1)}, u32[]{:S(2)}) copy-start(bf16[32,768]{1,0:T(8,128)(2,1)} %pre_hbm.1) | copy-start | bytes 147460
  3.4 0.8 %copy-start.2 = (bf16[32,768]{1,0:T(8,128)(2,1)S(1)}, bf16[32,768]{1,0:T(8,128)(2,1)}, u32[]{:S(2)}) copy-start(bf16[32,768]{1,0:T(8,128)(2,1)} %up_hbm.1) | copy-start | bytes 147460
  4.2 0.7 %copy-start.3 = (bf16[16,768]{1,0:T(8,128)(2,1)S(1)}, bf16[16,768]{1,0:T(8,128)(2,1)}, u32[]{:S(2)}) copy-start(bf16[16,768]{1,0:T(8,128)(2,1)} %fwd_hbm.1) | copy-start | bytes 73732
  4.9 0.7 %copy-start.4 = (bf16[16,768]{1,0:T(8,128)(2,1)S(1)}, bf16[16,768]{1,0:T(8,128)(2,1)}, u32[]{:S(2)}) copy-start(bf16[16,768]{1,0:T(8,128)(2,1)} %bwd_hbm.1) | copy-start | bytes 73732

commit v2 on v0

v2 whole, which is shorter than its diff:
```python
import math

import jax
import jax.numpy as jnp
from jax import lax
from jax.experimental import pallas as pl
from jax.experimental.pallas import tpu as pltpu
from jax.sharding import PartitionSpec as P

gelu_scale = math.sqrt(2.0 / math.pi)
cubic_term = 0.044715
F32, BF16 = jnp.float32, jnp.bfloat16
MESH = pl.DeviceIdType.MESH
TILE = 256


def gelu_tanh(values):
    inner_arg = gelu_scale * (values + cubic_term * values * values * values)
    return 0.5 * values * (1.0 + jnp.tanh(inner_arg))


def gelu_slope(values):
    tangent = jnp.tanh(gelu_scale * (values + cubic_term * values * values * values))
    return 0.5 * (1.0 + tangent) + 0.5 * values * (1.0 - tangent * tangent) * gelu_scale * (
        1.0 + 3.0 * cubic_term * values * values
    )


def flip(i, k):
    if k == 1:
        return i + 1 - 2 * lax.rem(i, 2)
    if k == 2:
        return lax.rem(i + 2, 4)
    return 3 - i


class Sems:
    def __init__(self, send, recv):
        self.send, self.recv, self.n = send, recv, 0

    def pair(self):
        self.n += 1
        return self.send.at[self.n - 1], self.recv.at[self.n - 1]


N_LOCAL = 6
N_REMOTE = 96


def kernel(
    fwd_hbm, bwd_hbm, w_hbm, bias_hbm, pre_hbm, up_hbm,
    hidden_ref, igrad_ref, wgrad_ref, bgrad_ref,
    xf, xb, g, q, w, bias, pre, up,
    p, core_out, core_in, x_out, x_in, y_out, y_in,
    rs_out, rs_in, line_out, line_in, sums,
    local_sem, send_sem, recv_sem,
):
    row, col = lax.axis_index("row"), lax.axis_index("col")
    yh, x, core = row // 8, lax.rem(row // 2, 4), lax.rem(row, 2)
    yl, z = col // 8, lax.rem(col, 8)
    mate, opposite = flip(yl, 1), 1 - yl // 2

    def device(yh=yh, x=x, core=core, yl=yl, z=z):
        return (yh * 8 + x * 2 + core, yl * 8 + z)

    near_z = (device(z=lax.rem(z + 1, 8)), device(z=lax.rem(z + 7, 8)))
    near_x = [device(x=flip(x, k)) for k in (1, 2, 3)]
    near_y = [device(yl=flip(yl, k)) for k in (1, 2, 3)]
    far_y = device(yh=1 - yh)
    twin = device(core=1 - core)
    near_row = [*near_x, twin, *[device(x=flip(x, k), core=1 - core) for k in (1, 2, 3)]]
    partners = [*near_z, *near_y, far_y, *near_row]

    sems = Sems(send_sem, recv_sem)
    started = []

    def copy(src, dst, target):
        s, r = sems.pair()
        c = pltpu.make_async_remote_copy(
            src_ref=src, dst_ref=dst, send_sem=s, recv_sem=r,
            device_id=target, device_id_type=MESH,
        )
        started.append(c)
        c.start()
        return c

    def at_z(at):
        return at // 4, lax.rem(at // 2, 2), lax.rem(at, 2)

    loads = [
        pltpu.make_async_copy(src, dst, local_sem.at[i])
        for i, (src, dst) in enumerate(
            [
                (fwd_hbm, xf.at[(yl, *at_z(z))]), (pre_hbm, pre), (up_hbm, up), (w_hbm, w),
                (bwd_hbm, xb.at[(yl, *at_z(z))]), (bias_hbm, bias),
            ]
        )
    ]
    barrier = pltpu.get_barrier_semaphore()
    for d in partners:
        pl.semaphore_signal(barrier, inc=1, device_id=d, device_id_type=MESH)
    for c in loads:
        c.start()
    pl.semaphore_wait(barrier, len(partners))

    class Gather:
        def __init__(self, hbm, ref):
            self.hbm, self.ref = hbm, ref
            self.hops = ((4, 3), (3, 4), (4, 3)) if ref is xf else ((3, 4), (4, 3), (3, 4))
            self.sent = {}

        def line(self):
            block = self.ref.at[(yl, *at_z(z))]
            self.lines = [copy(self.hbm, block, d) for d in near_y]

        def chunk(self, which, at):
            rows = (pl.ds(yl, 1), pl.ds(mate, 1), pl.ds(2 * opposite, 2))[which]
            return self.ref.at[(rows, *at_z(at))]

        def step(self, s, which):
            if s == 0 and which == 1:
                self.lines[0].wait_recv()
            if s == 0 and which == 2:
                self.lines[1].wait_recv()
                self.lines[2].wait_recv()
            for way in (0, 1):
                if s >= self.hops[which][way]:
                    continue
                if s > 0:
                    self.sent[s - 1, which, way].wait_recv()
                source = lax.rem(z - s + 8, 8) if way == 0 else lax.rem(z + s, 8)
                block = self.chunk(which, source)
                if s == 0 and which == 0:
                    src = self.hbm
                    block = self.ref.at[(yl, *at_z(z))]
                else:
                    src = block
                self.sent[s, which, way] = copy(src, block, near_z[way])

        def finish(self):
            for which in (0, 1, 2):
                for way in (0, 1):
                    self.sent[self.hops[which][way] - 1, which, way].wait_recv()

    fwd, bwd = Gather(fwd_hbm, xf), Gather(bwd_hbm, xb)

    def gather_grad():
        grad = (up[...].astype(F32) * gelu_slope(pre[...].astype(F32))).astype(BF16)
        g[yh, x, core] = grad

    def spread_grad(at):
        return [copy(g.at[at, x, core], g.at[at, x, core], d) for d in near_row]

    rs_hops = ((4, 3), (3, 4))
    rs_sent = {}
    slot_of = {}
    for part in (0, 1):
        for way in (0, 1):
            for s in range(rs_hops[part][way]):
                slot_of[s, part, way] = len(slot_of)
    halves = (yh, 1 - yh)

    def back_half(part):
        j = halves[part]
        rows = g[j].reshape(256, 768)

        def body(n, carry):
            at = pl.ds(pl.multiple_of(n * TILE, TILE), TILE)
            q[pl.ds(2 * j, 2), :, :, at] = lax.dot_general(
                rows, w[at, :], (((1,), (1,)), ((), ())), preferred_element_type=F32
            ).reshape(2, 8, 16, TILE)
            return carry

        lax.fori_loop(0, 3, body, 0)

    def rs_step(s, part):
        for way in (0, 1):
            hops = rs_hops[part][way]
            if s >= hops:
                continue
            left = hops - s
            target = lax.rem(z + left, 8) if way == 0 else lax.rem(z - left + 8, 8)
            value = q[pl.ds(2 * halves[part], 2), target]
            if s > 0:
                rs_sent[s - 1, part, way].wait_recv()
                value = value + rs_in[slot_of[s - 1, part, way]].astype(F32)
            slot = slot_of[s, part, way]
            rs_out[slot] = value.astype(BF16)
            rs_sent[s, part, way] = copy(rs_out.at[slot], rs_in.at[slot], near_z[way])

    def rs_end(part):
        value = q[pl.ds(2 * halves[part], 2), z]
        for way in (0, 1):
            s = rs_hops[part][way] - 1
            rs_sent[s, part, way].wait_recv()
            value = value + rs_in[slot_of[s, part, way]].astype(F32)
        q[pl.ds(2 * halves[part], 2), z] = value

    f_halves = (1 - yh, yh)

    def forward_half(part):
        j = f_halves[part]
        rows = xf[pl.ds(2 * j, 2)].reshape(256, 768)

        def body(n, carry):
            at = pl.ds(pl.multiple_of(n * TILE, TILE), TILE)
            p[part, :, :, :, at] = jnp.dot(rows, w[:, at], preferred_element_type=F32).reshape(4, 2, 32, TILE)
            return carry

        lax.fori_loop(0, 3, body, 0)
        core_out[part] = p[part, :, 1 - core].astype(BF16)
        return copy(core_out.at[part], core_in.at[part], twin)

    def forward_x(part, from_twin):
        from_twin.wait_recv()
        copies = []
        for k in (1, 2, 3):
            there = flip(x, k)
            x_out[part, k - 1] = (p[part, there, core] + core_in[part, there].astype(F32)).astype(BF16)
            copies.append(copy(x_out.at[part, k - 1], x_in.at[part, k - 1], near_x[k - 1]))
        sums[part] = p[part, x, core] + core_in[part, x].astype(F32)
        return copies

    def forward_sum(part, copies):
        for c in copies:
            c.wait_recv()
        return sums[part] + x_in[part, 0].astype(F32) + x_in[part, 1].astype(F32) + x_in[part, 2].astype(F32)

    fwd.line()
    fwd.step(0, 0)
    bwd.line()
    loads[1].wait()
    loads[2].wait()
    gather_grad()
    g_far = copy(g.at[yh, x, core], g.at[yh, x, core], far_y)
    g_here = spread_grad(yh)
    bwd.step(0, 0)
    fwd.step(1, 0)
    fwd.step(0, 1)
    fwd.step(0, 2)
    loads[3].wait()
    for c in g_here:
        c.wait_recv()
    back_half(0)
    rs_step(0, 0)
    fwd.step(2, 0)
    fwd.step(1, 1)
    fwd.step(1, 2)
    g_far.wait_recv()
    g_there = spread_grad(1 - yh)
    fwd.step(3, 0)
    rs_step(1, 0)
    fwd.step(2, 1)
    fwd.step(2, 2)
    bwd.step(1, 0)
    bwd.step(0, 1)
    bwd.step(0, 2)
    for c in g_there:
        c.wait_recv()
    back_half(1)
    rs_step(0, 1)
    fwd.step(3, 1)
    fwd.step(3, 2)
    rs_step(2, 0)
    bwd.step(2, 0)
    for c in loads:
        if c is not loads[1] and c is not loads[2] and c is not loads[3]:
            c.wait()
    fwd.finish()
    twin_0 = forward_half(0)
    rs_step(1, 1)
    bwd.step(1, 1)
    bwd.step(1, 2)
    twin_1 = forward_half(1)
    x_0 = forward_x(0, twin_0)
    rs_step(3, 0)
    bwd.step(3, 0)
    x_1 = forward_x(1, twin_1)
    rs_step(2, 1)
    bwd.step(2, 1)
    bwd.step(2, 2)
    y_out[...] = forward_sum(0, x_0).astype(BF16)
    far = copy(y_out, y_in, far_y)
    rs_end(0)
    bgrad_ref[...] = jnp.sum(g[...].reshape(512, 768).astype(F32), axis=0)
    rs_step(3, 1)
    bwd.step(3, 1)
    bwd.step(3, 2)
    sums[1] = forward_sum(1, x_1)
    rs_end(1)
    l_copies = []
    for k in (1, 2, 3):
        line_out[k - 1] = q[flip(yl, k), z].astype(BF16)
        l_copies.append(copy(line_out.at[k - 1], line_in.at[k - 1], near_y[k - 1]))
    bwd.finish()

    def w_body(n, carry):
        at = pl.ds(pl.multiple_of(n * TILE, TILE), TILE)
        wgrad_ref[at, :] = lax.dot_general(
            xb[:, :, :, :, :, at].reshape(512, TILE), g[...].reshape(512, 768), (((0,), (0,)), ((), ())),
            preferred_element_type=F32,
        )
        return carry

    lax.fori_loop(0, 3, w_body, 0)

    far.wait_recv()
    hidden_ref[...] = gelu_tanh(sums[1] + y_in[...].astype(F32) + bias[...]).astype(BF16)
    for c in l_copies:
        c.wait_recv()
    igrad_ref[...] = (
        q[yl, z] + line_in[0].astype(F32) + line_in[1].astype(F32) + line_in[2].astype(F32)
    ).astype(BF16)
    for c in started:
        c.wait_send()


def local(tokens_fwd, tokens_bwd, weight, bias, preact, upstream):
    hbm = pl.BlockSpec(memory_space=pltpu.HBM)
    vmem = pl.BlockSpec(memory_space=pltpu.VMEM)
    shapes = (
        jax.ShapeDtypeStruct((32, 768), BF16),
        jax.ShapeDtypeStruct((16, 768), BF16),
        jax.ShapeDtypeStruct((768, 768), F32),
        jax.ShapeDtypeStruct((768,), F32),
    )
    tokens_fwd, tokens_bwd, weight, bias, preact, upstream = [
        pltpu.with_memory_space_constraint(a, pltpu.HBM)
        for a in (tokens_fwd, tokens_bwd, weight, bias, preact, upstream)
    ]
    return pl.pallas_call(
        kernel,
        out_shape=shapes,
        in_specs=[hbm] * 6,
        out_specs=[vmem] * 4,
        scratch_shapes=[
            pltpu.VMEM((4, 2, 2, 2, 16, 768), BF16),
            pltpu.VMEM((4, 2, 2, 2, 16, 768), BF16),
            pltpu.VMEM((2, 4, 2, 32, 768), BF16),
            pltpu.VMEM((4, 8, 16, 768), F32),
            pltpu.VMEM((768, 768), BF16),
            pltpu.VMEM((768,), F32),
            pltpu.VMEM((32, 768), BF16),
            pltpu.VMEM((32, 768), BF16),
            pltpu.VMEM((2, 4, 2, 32, 768), F32),
            pltpu.VMEM((2, 4, 32, 768), BF16),
            pltpu.VMEM((2, 4, 32, 768), BF16),
            pltpu.VMEM((2, 3, 32, 768), BF16),
            pltpu.VMEM((2, 3, 32, 768), BF16),
            pltpu.VMEM((32, 768), BF16),
            pltpu.VMEM((32, 768), BF16),
            pltpu.VMEM((14, 2, 16, 768), BF16),
            pltpu.VMEM((14, 2, 16, 768), BF16),
            pltpu.VMEM((3, 16, 768), BF16),
            pltpu.VMEM((3, 16, 768), BF16),
            pltpu.VMEM((2, 32, 768), F32),
            pltpu.SemaphoreType.DMA((N_LOCAL,)),
            pltpu.SemaphoreType.DMA((N_REMOTE,)),
            pltpu.SemaphoreType.DMA((N_REMOTE,)),
        ],
        compiler_params=pltpu.CompilerParams(
            collective_id=0, has_side_effects=True, vmem_limit_bytes=48 * 2**20
        ),
        cost_estimate=pl.CostEstimate(flops=3 * 2 * 512 * 768 * 768, bytes_accessed=8 * 2**20, transcendentals=50000),
        name="feed_forward",
    )(tokens_fwd, tokens_bwd, weight, bias, preact, upstream)

def solution(mesh):
    return jax.shard_map(
        local,
        mesh=mesh,
        in_specs=(
            P("col", "row"),
            P("col", "row"),
            P("row", "col"),
            P("col"),
            P("row", "col"),
            P("row", "col"),
        ),
        out_specs=(P("row", "col"), P("col", "row"), P("row", "col"), P("col")),
        check_vma=False,
    )
```

time: 355 us -> 56 us (0.16)
  the two profiles are of different devices: /device:TPU:6 before, /device:TPU:1 now
where the time goes in v2:
time: 56 us; the launch traced here: 55.9 us
  Pallas kernels  52 us (93%)
  local copies, waits for them, and re-layouts  3.23 us (6%)
  between operations  0.64 us (1%)
    pallas_call x1, Pallas kernels, local(): pl.pallas_call(kernel, out_shape=shapes, in_specs=[hbm] * 6, out_specs=[v...  52 us
    unnamed x4, local copies, waits for them, and re-layouts  3.23 us

profile of v2, /device:TPU:1, one launch (start us, length us, event | category | flops | bytes accessed | tf_op | source)
XLA Modules:
  0.0 55.9 jit_solution(12782873719491471618)
XLA Ops:
  0.6 52.0 %feed_forward.1 = (bf16[32,768]{1,0:T(8,128)(2,1)S(1)}, bf16[16,768]{1,0:T(8,128)(2,1)S(1)}, f32[768,768]{1,0:T(8,128)S(1)}, f32[768]{0:T(1024)S(1)}) custom-call(bf16[16,768]{1,0:T(8,128)(2,1)} %fwd_hbm.1, bf16[16,768]{1,0:T(8,128)(2,1)} %bwd_hbm.1, bf16[768,768]{1,0:T(8,128)(2,1)} %w_hbm.1, f32[768]{0:T(1024)} %bias_hbm.1, bf16[32,768]{1,0:T(8,128)(2,1)} %pre_hbm.1, ...), custom_call_target="tpu_custom_call" | custom-call | flops 1811939328 | bytes 8388608 | tf_op jit(solution)/shard_map/feed_forward/pallas_call | solution.py:331
  52.7 0.6 %copy.14 = bf16[32,768]{1,0:T(8,128)(2,1)} copy(bf16[32,768]{1,0:T(8,128)(2,1)S(1)} %get-tuple-element.8) | data formatting | bytes 98304
  53.3 0.6 %copy.15 = bf16[16,768]{1,0:T(8,128)(2,1)} copy(bf16[16,768]{1,0:T(8,128)(2,1)S(1)} %get-tuple-element.9) | data formatting | bytes 49152
  53.9 1.4 %copy.16 = f32[768,768]{1,0:T(8,128)} copy(f32[768,768]{1,0:T(8,128)S(1)} %get-tuple-element.10) | data formatting | bytes 4718592
  55.3 0.6 %copy.17 = f32[768]{0:T(1024)} copy(f32[768]{0:T(1024)S(1)} %get-tuple-element.11) | data formatting | bytes 6144

commit v3 on v0

v3 whole, which is shorter than its diff:
```python
import math

import jax
import jax.numpy as jnp
from jax import lax
from jax.experimental import pallas as pl
from jax.experimental.pallas import tpu as pltpu
from jax.sharding import PartitionSpec as P

gelu_scale = math.sqrt(2.0 / math.pi)
cubic_term = 0.044715
F32, BF16 = jnp.float32, jnp.bfloat16
MESH = pl.DeviceIdType.MESH
TILE = 256


def gelu_tanh(values):
    inner_arg = gelu_scale * (values + cubic_term * values * values * values)
    return 0.5 * values * (1.0 + jnp.tanh(inner_arg))


def gelu_slope(values):
    tangent = jnp.tanh(gelu_scale * (values + cubic_term * values * values * values))
    return 0.5 * (1.0 + tangent) + 0.5 * values * (1.0 - tangent * tangent) * gelu_scale * (
        1.0 + 3.0 * cubic_term * values * values
    )


def flip(i, k):
    if k == 1:
        return i + 1 - 2 * lax.rem(i, 2)
    if k == 2:
        return lax.rem(i + 2, 4)
    return 3 - i


class Sems:
    def __init__(self, send, recv):
        self.send, self.recv, self.n = send, recv, 0

    def pair(self):
        self.n += 1
        return self.send.at[self.n - 1], self.recv.at[self.n - 1]


ORDER = (
    ("b", 0, 0, 0), ("f", "line"), ("f", 0, 0, 0), ("far",), ("f", 0, 1, 0), ("spread", 0), ("b", 1, 0, 0),
    ("b", 1, 0, 1), ("f", 0, 2, 0), ("f", 1, 1, 1), ("f", 1, 0, 1), ("spread", 1), ("b", "line"), ("f", 1, 1, 0),
    ("f", 1, 0, 0), ("f", 1, 2, 1), ("f", 1, 2, 0), ("back", 0), ("rs", 0, 0, 1), ("rs", 0, 0, 0), ("back", 1),
    ("rs", 0, 1, 0), ("rs", 0, 1, 1), ("fwd", 0), ("rs", 1, 0, 1), ("rs", 1, 0, 0), ("rs", 1, 1, 0), ("rs", 1, 1, 1),
    ("fwd", 1), ("fsum", 0), ("rsend", 0), ("rsend", 1), ("rsline",), ("wg",), ("fsum", 1), ("bg",), ("hid",),
    ("igrad",),
)

RS_SLOT = {"three": 0, "four": 2, "one": 3, "two": 5}
RS_SIZE = {"three": 2, "four": 1, "one": 2, "two": 2}
N_LOCAL = 6
N_REMOTE = 112


def kernel(
    fwd_hbm, bwd_hbm, w_hbm, bias_hbm, pre_hbm, up_hbm,
    hidden_ref, igrad_ref, wgrad_ref, bgrad_ref,
    xf, xb, g, q, w, bias, pre, up,
    p, x_out, x_in, y_out, y_in,
    rs_out, rs_in, line_out, line_in, sums,
    local_sem, send_sem, recv_sem,
):
    row, col = lax.axis_index("row"), lax.axis_index("col")
    yh, x, core = row // 8, lax.rem(row // 2, 4), lax.rem(row, 2)
    yl, z = col // 8, lax.rem(col, 8)
    mate, opposite = flip(yl, 1), 1 - yl // 2

    def device(yh=yh, x=x, core=core, yl=yl, z=z):
        return (yh * 8 + x * 2 + core, yl * 8 + z)

    along_z = {away: device(z=lax.rem(z + away + 8, 8)) for away in (1, -1, 2, -2)}
    near_z = (along_z[1], along_z[-1])
    near_y = [device(yl=flip(yl, k)) for k in (1, 2, 3)]
    far_y = device(yh=1 - yh)
    row_places = [(flip(x, k) if k else x, c) for k, c in ((2, 1 - core), (2, core), (1, 1 - core), (3, 1 - core), (1, core), (3, core), (0, 1 - core))]
    near_row = [device(x=there, core=c) for there, c in row_places]
    partners = [*along_z.values(), *near_y, far_y, *near_row]

    sems = Sems(send_sem, recv_sem)
    started = []

    def copy(src, dst, target):
        s, r = sems.pair()
        c = pltpu.make_async_remote_copy(
            src_ref=src, dst_ref=dst, send_sem=s, recv_sem=r,
            device_id=target, device_id_type=MESH,
        )
        started.append(c)
        c.start()
        return c

    def at_z(at):
        return at // 4, lax.rem(at // 2, 2), lax.rem(at, 2)

    loads = [
        pltpu.make_async_copy(src, dst, local_sem.at[i])
        for i, (src, dst) in enumerate(
            [
                (fwd_hbm, xf.at[(yl, *at_z(z))]), (pre_hbm, pre), (up_hbm, up), (w_hbm, w),
                (bwd_hbm, xb.at[(yl, *at_z(z))]), (bias_hbm, bias),
            ]
        )
    ]
    barrier = pltpu.get_barrier_semaphore()
    for d in partners:
        pl.semaphore_signal(barrier, inc=1, device_id=d, device_id_type=MESH)
    for c in loads:
        c.start()
    loads[1].wait()
    loads[2].wait()
    g[yh, x, core] = (up[...].astype(F32) * gelu_slope(pre[...].astype(F32))).astype(BF16)
    pl.semaphore_wait(barrier, len(partners))

    waited = {1, 2}

    def arrived(*copies):
        for c in copies:
            if id(c) not in waited:
                waited.add(id(c))
                c.wait_recv()

    def loaded(*which):
        for i in which:
            if i not in waited:
                waited.add(i)
                loads[i].wait()

    class Gather:
        def __init__(self, hbm, ref, hops, two, z_first=False):
            self.hbm, self.ref, self.hops, self.two, self.z_first = hbm, ref, hops, two, z_first
            self.sent = {}

        def line(self):
            if self.z_first:
                arrived(*self.sent.values())
                loaded(4)
                block = self.ref.at[yl]
                self.lines = [copy(block, block, d) for d in near_y]
                return
            block = self.ref.at[(yl, *at_z(z))]
            self.lines = [copy(self.hbm, block, d) for d in near_y]

        def first(self, which):
            return [(self.lines[0],), self.lines[1:]][which - 1] if which else ()

        def near(self, which):
            arrived(*self.first(which))
            block = self.block(which, z)
            src = self.hbm if which == 0 else block
            for away in (2, 1):
                for way in (0, 1):
                    self.sent[away, which, way] = copy(src, block, along_z[(away, -away)[way]])

        def far(self, which, way):
            arrived(self.sent[2, which, way])
            sign = (1, -1)[way]
            source = lax.rem(z - 2 * sign + 8, 8)
            if which == 2:
                half = self.ref.at[(2 * opposite + way, *at_z(source))]
                self.sent[4, which, way] = copy(half, half, along_z[2 * sign])
            elif which == way:
                block = self.block(which, source)
                self.sent[4, which, way] = copy(block, block, along_z[2 * sign])
            block = self.block(which, source)
            self.sent[3, which, way] = copy(block, block, along_z[sign])

        def block(self, which, source):
            if which == 0:
                return self.ref.at[(yl, *at_z(source))]
            rows = pl.ds(mate, 1) if which == 1 else pl.ds(2 * opposite, 2)
            return self.ref.at[(rows, *at_z(source))]

        def step(self, s, which, way):
            if self.two:
                return self.far(which, way) if s else self.near(which)
            source = lax.rem(z - s + 8, 8) if way == 0 else lax.rem(z + s, 8)
            if which == 0:
                block = self.ref.at[(yl, *at_z(source))]
            else:
                rows = pl.ds(mate, 1) if which == 1 else pl.ds(2 * opposite, 2)
                block = self.ref.at[(rows, *at_z(source))]
            if s > 0:
                arrived(self.sent[s - 1, which, way])
            elif which == 1:
                arrived(self.lines[0])
            elif which == 2:
                arrived(*self.lines[1:])
            src = self.hbm if s == 0 and which == 0 else block
            self.sent[s, which, way] = copy(src, block, near_z[way])

        def finish(self):
            if self.z_first:
                arrived(*self.lines)
                return
            if self.two:
                arrived(*self.sent.values())
                return
            for which in (0, 1, 2):
                for way in (0, 1):
                    arrived(self.sent[self.hops[which][way] - 1, which, way])

    gathers = {
        "f": Gather(fwd_hbm, xf, ((4, 3), (3, 4), (4, 3)), True),
        "b": Gather(bwd_hbm, xb, ((3, 4), (4, 3), (3, 4)), True, True),
    }
    sent = {}

    def far():
        sent["far"] = copy(g.at[yh, x, core], g.at[yh, x, core], far_y)

    def spread(half):
        if half == 1:
            arrived(sent["far"])
        at = (yh, 1 - yh)[half]
        sent["spread", half] = [copy(g.at[at, x, core], g.at[at, x, core], d) for d in near_row]

    halves = (yh, 1 - yh)

    def back(part):
        arrived(*sent["spread", part])
        loaded(3)
        j = halves[part]
        rows = g[j].reshape(256, 768)

        def body(n, carry):
            at = pl.ds(pl.multiple_of(n * TILE, TILE), TILE)
            q[pl.ds(2 * j, 2), :, :, at] = lax.dot_general(
                rows, w[at, :], (((1,), (1,)), ((), ())), preferred_element_type=F32
            ).reshape(2, 8, 16, TILE)
            return carry

        lax.fori_loop(0, 3, body, 0)

    def rs_send(name, part, way, value, away):
        slots = pl.ds(RS_SLOT[name] + 7 * (2 * part + way), value.shape[0])
        rs_out[slots] = value.astype(BF16)
        sent[name, part, way] = copy(rs_out.at[slots], rs_in.at[slots], along_z[away])

    def rs_got(name, part, way):
        arrived(sent[name, part, way])
        slots = pl.ds(RS_SLOT[name] + 7 * (2 * part + way), RS_SIZE[name])
        return rs_in[slots].astype(F32)

    def rs(s, part, way):
        j, sign = halves[part], (1, -1)[way]

        def sums_for(away):
            return q[pl.ds(2 * j, 2), lax.rem(z + sign * away + 8, 8)]

        if s == 0:
            rs_send("three", part, way, sums_for(3), sign)
            rs_send("four", part, way, q[pl.ds(2 * j + way, 1), lax.rem(z + 4, 8)], 2 * sign)
            rs_send("one", part, way, sums_for(1), sign)
        else:
            value = sums_for(2) + rs_got("three", part, way)
            more = rs_got("four", part, way)
            parts = [value[:1] + more, value[1:]] if way == 0 else [value[:1], value[1:] + more]
            rs_send("two", part, way, jnp.concatenate(parts, axis=0), 2 * sign)

    def rsend(part):
        value = q[pl.ds(2 * halves[part], 2), z]
        for way in (0, 1):
            value = value + rs_got("one", part, way) + rs_got("two", part, way)
        q[pl.ds(2 * halves[part], 2), z] = value

    def rsline():
        sent["line"] = []
        for k in (1, 2, 3):
            line_out[k - 1] = q[flip(yl, k), z].astype(BF16)
            sent["line"].append(copy(line_out.at[k - 1], line_in.at[k - 1], near_y[k - 1]))

    def igrad():
        arrived(*sent["line"])
        igrad_ref[...] = (
            q[yl, z] + line_in[0].astype(F32) + line_in[1].astype(F32) + line_in[2].astype(F32)
        ).astype(BF16)

    f_halves = (1 - yh, yh)

    def fwd(part):
        gathers["f"].finish()
        loaded(0, 3)
        j = f_halves[part]
        rows = xf[pl.ds(2 * j, 2)].reshape(256, 768)

        def body(n, carry):
            at = pl.ds(pl.multiple_of(n * TILE, TILE), TILE)
            value = jnp.dot(rows, w[:, at], preferred_element_type=F32).reshape(4, 2, 32, TILE)
            p[part, :, :, :, at] = value
            x_out[part, :, :, :, at] = value.astype(BF16)
            return carry

        lax.fori_loop(0, 3, body, 0)
        sent["x", part] = [
            copy(x_out.at[part, there, c], x_in.at[part, i], d)
            for i, ((there, c), d) in enumerate(zip(row_places, near_row))
        ]

    def fsum(part):
        arrived(*sent["x", part])
        value = p[part, x, core]
        for i in range(7):
            value = value + x_in[part, i].astype(F32)
        if part == 0:
            y_out[...] = value.astype(BF16)
            sent["y"] = copy(y_out, y_in, far_y)
        else:
            sums[...] = value

    def hid():
        loaded(5)
        arrived(sent["y"])
        hidden_ref[...] = gelu_tanh(sums[...] + y_in[...].astype(F32) + bias[...]).astype(BF16)

    def bg():
        bgrad_ref[...] = jnp.sum(g[...].reshape(512, 768).astype(F32), axis=0)

    def wg():
        gathers["b"].finish()
        loaded(4)

        def body(n, carry):
            at = pl.ds(pl.multiple_of(n * TILE, TILE), TILE)
            wgrad_ref[at, :] = lax.dot_general(
                xb[:, :, :, :, :, at].reshape(512, TILE), g[...].reshape(512, 768), (((0,), (0,)), ((), ())),
                preferred_element_type=F32,
            )
            return carry

        lax.fori_loop(0, 3, body, 0)

    single = dict(
        far=far, spread=spread, back=back, rs=rs, rsend=rsend, rsline=rsline, igrad=igrad,
        fwd=fwd, fsum=fsum, hid=hid, bg=bg, wg=wg,
    )
    for what, *at in ORDER:
        if what in gathers:
            if at == ["line"]:
                gathers[what].line()
            else:
                gathers[what].step(*at)
        else:
            single[what](*at)
    for c in started:
        c.wait_send()


def local(tokens_fwd, tokens_bwd, weight, bias, preact, upstream):
    hbm = pl.BlockSpec(memory_space=pltpu.HBM)
    vmem = pl.BlockSpec(memory_space=pltpu.VMEM)
    shapes = (
        jax.ShapeDtypeStruct((32, 768), BF16),
        jax.ShapeDtypeStruct((16, 768), BF16),
        jax.ShapeDtypeStruct((768, 768), F32),
        jax.ShapeDtypeStruct((768,), F32),
    )
    tokens_fwd, tokens_bwd, weight, bias, preact, upstream = [
        pltpu.with_memory_space_constraint(a, pltpu.HBM)
        for a in (tokens_fwd, tokens_bwd, weight, bias, preact, upstream)
    ]
    return pl.pallas_call(
        kernel,
        out_shape=shapes,
        in_specs=[hbm] * 6,
        out_specs=[vmem] * 4,
        scratch_shapes=[
            pltpu.VMEM((4, 2, 2, 2, 16, 768), BF16),
            pltpu.VMEM((4, 2, 2, 2, 16, 768), BF16),
            pltpu.VMEM((2, 4, 2, 32, 768), BF16),
            pltpu.VMEM((4, 8, 16, 768), F32),
            pltpu.VMEM((768, 768), BF16),
            pltpu.VMEM((768,), F32),
            pltpu.VMEM((32, 768), BF16),
            pltpu.VMEM((32, 768), BF16),
            pltpu.VMEM((2, 4, 2, 32, 768), F32),
            pltpu.VMEM((2, 4, 2, 32, 768), BF16),
            pltpu.VMEM((2, 7, 32, 768), BF16),
            pltpu.VMEM((32, 768), BF16),
            pltpu.VMEM((32, 768), BF16),
            pltpu.VMEM((28, 16, 768), BF16),
            pltpu.VMEM((28, 16, 768), BF16),
            pltpu.VMEM((3, 16, 768), BF16),
            pltpu.VMEM((3, 16, 768), BF16),
            pltpu.VMEM((32, 768), F32),
            pltpu.SemaphoreType.DMA((N_LOCAL,)),
            pltpu.SemaphoreType.DMA((N_REMOTE,)),
            pltpu.SemaphoreType.DMA((N_REMOTE,)),
        ],
        compiler_params=pltpu.CompilerParams(
            collective_id=0, has_side_effects=True, vmem_limit_bytes=48 * 2**20
        ),
        cost_estimate=pl.CostEstimate(flops=3 * 2 * 512 * 768 * 768, bytes_accessed=8 * 2**20, transcendentals=50000),
        name="feed_forward",
    )(tokens_fwd, tokens_bwd, weight, bias, preact, upstream)

def solution(mesh):
    return jax.shard_map(
        local,
        mesh=mesh,
        in_specs=(
            P("col", "row"),
            P("col", "row"),
            P("row", "col"),
            P("col"),
            P("row", "col"),
            P("row", "col"),
        ),
        out_specs=(P("row", "col"), P("col", "row"), P("row", "col"), P("col")),
        check_vma=False,
    )
```

time: 355 us -> 51 us (0.14)
  blocking collectives: 239 us -> 0 us
  waiting for transfers between devices: 87.9 us -> 0 us
  Pallas kernels: 0 us -> 46.8 us
  between operations: 14.1 us -> 0.64 us
  matrix products: 5.84 us -> 0 us
  other arithmetic: 3.86 us -> 0 us
    all_gather x3 -> x0, blocking collectives: 194 us -> none  [the longest x1 89.5 us: local(): lax.all_gather(tokens_fwd, 'col', axis=0, tiled=True)]
    reduce_scatter x2 -> x0, waiting for transfers between devices: 87.8 us -> none  [the longest x1 87.8 us: local(): lax.psum_scatter(lax.dot_general(piece, weight, (((1,), (1,)), ((), ())),...]
    pallas_call x0 -> x1, Pallas kernels: none -> 46.8 us  [local(): pl.pallas_call(kernel, out_shape=shapes, in_specs=[hbm] * 6, out_specs=[v...]
    psum x1 -> x0, blocking collectives: 44.5 us -> none  [local(): bias_grad = lax.psum(jnp.sum(own_grad.astype(jnp.float32), axis=0), 'row')]
    dot_general x3 -> x0, matrix products: 5.84 us -> none  [the longest x1 1.96 us: local(): lax.dot_general(piece, weight, (((1,), (1,)), ((), ())), preferred_elemen...]
  transfers between devices with their start and end apart: 2 -> 0, of which waited for: 1 -> 0; matrix products, arithmetic and copies ran while one was open for 2% -> 0% of each run, Pallas kernels for 0% -> 0%
where the time goes in v3:
time: 51 us; the launch traced here: 50.7 us
  Pallas kernels  46.8 us (92%)
  local copies, waits for them, and re-layouts  3.23 us (6%)
  between operations  0.64 us (1%)
    pallas_call x1, Pallas kernels, local(): pl.pallas_call(kernel, out_shape=shapes, in_specs=[hbm] * 6, out_specs=[v...  46.8 us
    unnamed x4, local copies, waits for them, and re-layouts  3.23 us

profile of v3, /device:TPU:6, one launch (start us, length us, event | category | flops | bytes accessed | tf_op | source)
XLA Modules:
  0.0 50.7 jit_solution(15059597598404324967)
XLA Ops:
  0.6 46.8 %feed_forward.1 = (bf16[32,768]{1,0:T(8,128)(2,1)S(1)}, bf16[16,768]{1,0:T(8,128)(2,1)S(1)}, f32[768,768]{1,0:T(8,128)S(1)}, f32[768]{0:T(1024)S(1)}) custom-call(bf16[16,768]{1,0:T(8,128)(2,1)} %fwd_hbm.1, bf16[16,768]{1,0:T(8,128)(2,1)} %bwd_hbm.1, bf16[768,768]{1,0:T(8,128)(2,1)} %w_hbm.1, f32[768]{0:T(1024)} %bias_hbm.1, bf16[32,768]{1,0:T(8,128)(2,1)} %pre_hbm.1, ...), custom_call_target="tpu_custom_call" | custom-call | flops 1811939328 | bytes 8388608 | tf_op jit(solution)/shard_map/feed_forward/pallas_call | solution.py:367
  47.4 0.6 %copy.14 = bf16[32,768]{1,0:T(8,128)(2,1)} copy(bf16[32,768]{1,0:T(8,128)(2,1)S(1)} %get-tuple-element.8) | data formatting | bytes 98304
  48.1 0.6 %copy.15 = bf16[16,768]{1,0:T(8,128)(2,1)} copy(bf16[16,768]{1,0:T(8,128)(2,1)S(1)} %get-tuple-element.9) | data formatting | bytes 49152
  48.7 1.4 %copy.16 = f32[768,768]{1,0:T(8,128)} copy(f32[768,768]{1,0:T(8,128)S(1)} %get-tuple-element.10) | data formatting | bytes 4718592
  50.1 0.6 %copy.17 = f32[768]{0:T(1024)} copy(f32[768]{0:T(1024)S(1)} %get-tuple-element.11) | data formatting | bytes 6144

commit v4 on v3

--- a/solution.py
+++ b/solution.py
@@ -34,13 +34,37 @@
     return 3 - i
 
 
-class Sems:
-    def __init__(self, send, recv):
-        self.send, self.recv, self.n = send, recv, 0
-
-    def pair(self):
-        self.n += 1
-        return self.send.at[self.n - 1], self.recv.at[self.n - 1]
+class Copies:
+    def __init__(self, extent, send, recv):
+        self.extent, self.send, self.recv = extent, send, recv
+        self.groups, self.waited, self.sent = {}, set(), 0
+
+    def start(self, src, dst, target, group):
+        rows = math.prod(dst.shape) // 768
+        number, before = self.groups.get(group, (len(self.groups), 0))
+        self.groups[group] = (number, before + rows)
+        self.sent += rows
+        pltpu.make_async_remote_copy(
+            src_ref=src, dst_ref=dst, send_sem=self.send, recv_sem=self.recv.at[number],
+            device_id=target, device_id_type=MESH,
+        ).start()
+
+    def whole(self, rows, number, target):
+        extent = self.extent.at[pl.ds(0, rows)]
+        return pltpu.make_async_remote_copy(
+            src_ref=extent, dst_ref=extent, send_sem=self.send, recv_sem=self.recv.at[number],
+            device_id=target, device_id_type=MESH,
+        )
+
+    def arrived(self, target, *groups):
+        for group in groups:
+            if group not in self.waited:
+                self.waited.add(group)
+                number, rows = self.groups[group]
+                self.whole(rows, number, target).wait_recv()
+
+    def finish(self, target):
+        self.whole(self.sent, 0, target).wait_send()
 
 
 ORDER = (
@@ -52,10 +76,12 @@
     ("igrad",),
 )
 
+
 RS_SLOT = {"three": 0, "four": 2, "one": 3, "two": 5}
 RS_SIZE = {"three": 2, "four": 1, "one": 2, "two": 2}
 N_LOCAL = 6
-N_REMOTE = 112
+N_GROUPS = 26
+SENT_ROWS = 2448
 
 
 def kernel(
@@ -64,7 +90,7 @@
     xf, xb, g, q, w, bias, pre, up,
     p, x_out, x_in, y_out, y_in,
     rs_out, rs_in, line_out, line_in, sums,
-    local_sem, send_sem, recv_sem,
+    extent, local_sem, send_sem, recv_sem,
 ):
     row, col = lax.axis_index("row"), lax.axis_index("col")
     yh, x, core = row // 8, lax.rem(row // 2, 4), lax.rem(row, 2)
@@ -82,18 +108,11 @@
     near_row = [device(x=there, core=c) for there, c in row_places]
     partners = [*along_z.values(), *near_y, far_y, *near_row]
 
-    sems = Sems(send_sem, recv_sem)
-    started = []
-
-    def copy(src, dst, target):
-        s, r = sems.pair()
-        c = pltpu.make_async_remote_copy(
-            src_ref=src, dst_ref=dst, send_sem=s, recv_sem=r,
-            device_id=target, device_id_type=MESH,
-        )
-        started.append(c)
-        c.start()
-        return c
+    copies = Copies(extent, send_sem, recv_sem)
+    copy = copies.start
+
+    def arrived(*groups):
+        copies.arrived(near_z[0], *groups)
 
     def at_z(at):
         return at // 4, lax.rem(at // 2, 2), lax.rem(at, 2)
@@ -119,12 +138,6 @@
 
     waited = {1, 2}
 
-    def arrived(*copies):
-        for c in copies:
-            if id(c) not in waited:
-                waited.add(id(c))
-                c.wait_recv()
-
     def loaded(*which):
         for i in which:
             if i not in waited:
@@ -132,43 +145,18 @@
                 loads[i].wait()
 
     class Gather:
-        def __init__(self, hbm, ref, hops, two, z_first=False):
-            self.hbm, self.ref, self.hops, self.two, self.z_first = hbm, ref, hops, two, z_first
-            self.sent = {}
+        def __init__(self, name, hbm, ref, z_first):
+            self.name, self.hbm, self.ref, self.z_first = name, hbm, ref, z_first
 
         def line(self):
             if self.z_first:
-                arrived(*self.sent.values())
+                arrived((self.name, "rest"))
                 loaded(4)
-                block = self.ref.at[yl]
-                self.lines = [copy(block, block, d) for d in near_y]
-                return
-            block = self.ref.at[(yl, *at_z(z))]
-            self.lines = [copy(self.hbm, block, d) for d in near_y]
-
-        def first(self, which):
-            return [(self.lines[0],), self.lines[1:]][which - 1] if which else ()
-
-        def near(self, which):
-            arrived(*self.first(which))
-            block = self.block(which, z)
-            src = self.hbm if which == 0 else block
-            for away in (2, 1):
-                for way in (0, 1):
-                    self.sent[away, which, way] = copy(src, block, along_z[(away, -away)[way]])
-
-        def far(self, which, way):
-            arrived(self.sent[2, which, way])
-            sign = (1, -1)[way]
-            source = lax.rem(z - 2 * sign + 8, 8)
-            if which == 2:
-                half = self.ref.at[(2 * opposite + way, *at_z(source))]
-                self.sent[4, which, way] = copy(half, half, along_z[2 * sign])
-            elif which == way:
-                block = self.block(which, source)
-                self.sent[4, which, way] = copy(block, block, along_z[2 * sign])
-            block = self.block(which, source)
-            self.sent[3, which, way] = copy(block, block, along_z[sign])
+                block = src = self.ref.at[yl]
+            else:
+                block, src = self.ref.at[(yl, *at_z(z))], self.hbm
+            for k in (1, 2, 3):
+                copy(src, block, near_y[k - 1], (self.name, "line", 0 if self.z_first else min(k, 2)))
 
         def block(self, which, source):
             if which == 0:
@@ -177,53 +165,44 @@
             return self.ref.at[(rows, *at_z(source))]
 
         def step(self, s, which, way):
-            if self.two:
-                return self.far(which, way) if s else self.near(which)
-            source = lax.rem(z - s + 8, 8) if way == 0 else lax.rem(z + s, 8)
-            if which == 0:
-                block = self.ref.at[(yl, *at_z(source))]
-            else:
-                rows = pl.ds(mate, 1) if which == 1 else pl.ds(2 * opposite, 2)
-                block = self.ref.at[(rows, *at_z(source))]
-            if s > 0:
-                arrived(self.sent[s - 1, which, way])
-            elif which == 1:
-                arrived(self.lines[0])
-            elif which == 2:
-                arrived(*self.lines[1:])
-            src = self.hbm if s == 0 and which == 0 else block
-            self.sent[s, which, way] = copy(src, block, near_z[way])
+            if s == 0:
+                if which:
+                    arrived((self.name, "line", which))
+                block = self.block(which, z)
+                src = block if which else self.hbm
+                for way in (0, 1):
+                    copy(src, block, along_z[(2, -2)[way]], (self.name, 2, which, way))
+                for way in (0, 1):
+                    copy(src, block, along_z[(1, -1)[way]], (self.name, "rest"))
+                return
+            arrived((self.name, 2, which, way))
+            sign = (1, -1)[way]
+            source = lax.rem(z - 2 * sign + 8, 8)
+            if which == 2 or which == way:
+                half = self.ref.at[(2 * opposite + way, *at_z(source))] if which == 2 else self.block(which, source)
+                copy(half, half, along_z[2 * sign], (self.name, "rest"))
+            block = self.block(which, source)
+            copy(block, block, along_z[sign], (self.name, "rest"))
 
         def finish(self):
-            if self.z_first:
-                arrived(*self.lines)
-                return
-            if self.two:
-                arrived(*self.sent.values())
-                return
-            for which in (0, 1, 2):
-                for way in (0, 1):
-                    arrived(self.sent[self.hops[which][way] - 1, which, way])
-
-    gathers = {
-        "f": Gather(fwd_hbm, xf, ((4, 3), (3, 4), (4, 3)), True),
-        "b": Gather(bwd_hbm, xb, ((3, 4), (4, 3), (3, 4)), True, True),
-    }
-    sent = {}
+            arrived((self.name, "line", 0) if self.z_first else (self.name, "rest"))
+
+    gathers = {"f": Gather("f", fwd_hbm, xf, False), "b": Gather("b", bwd_hbm, xb, True)}
 
     def far():
-        sent["far"] = copy(g.at[yh, x, core], g.at[yh, x, core], far_y)
+        copy(g.at[yh, x, core], g.at[yh, x, core], far_y, "far")
 
     def spread(half):
         if half == 1:
-            arrived(sent["far"])
+            arrived("far")
         at = (yh, 1 - yh)[half]
-        sent["spread", half] = [copy(g.at[at, x, core], g.at[at, x, core], d) for d in near_row]
+        for d in near_row:
+            copy(g.at[at, x, core], g.at[at, x, core], d, ("spread", half))
 
     halves = (yh, 1 - yh)
 
     def back(part):
-        arrived(*sent["spread", part])
+        arrived(("spread", part))
         loaded(3)
         j = halves[part]
         rows = g[j].reshape(256, 768)
@@ -237,15 +216,13 @@
 
         lax.fori_loop(0, 3, body, 0)
 
-    def rs_send(name, part, way, value, away):
+    def rs_send(name, part, way, value, away, group):
         slots = pl.ds(RS_SLOT[name] + 7 * (2 * part + way), value.shape[0])
         rs_out[slots] = value.astype(BF16)
-        sent[name, part, way] = copy(rs_out.at[slots], rs_in.at[slots], along_z[away])
+        copy(rs_out.at[slots], rs_in.at[slots], along_z[away], group)
 
     def rs_got(name, part, way):
-        arrived(sent[name, part, way])
-        slots = pl.ds(RS_SLOT[name] + 7 * (2 * part + way), RS_SIZE[name])
-        return rs_in[slots].astype(F32)
+        return rs_in[pl.ds(RS_SLOT[name] + 7 * (2 * part + way), RS_SIZE[name])].astype(F32)
 
     def rs(s, part, way):
         j, sign = halves[part], (1, -1)[way]
@@ -254,29 +231,30 @@
             return q[pl.ds(2 * j, 2), lax.rem(z + sign * away + 8, 8)]
 
         if s == 0:
-            rs_send("three", part, way, sums_for(3), sign)
-            rs_send("four", part, way, q[pl.ds(2 * j + way, 1), lax.rem(z + 4, 8)], 2 * sign)
-            rs_send("one", part, way, sums_for(1), sign)
+            rs_send("three", part, way, sums_for(3), sign, ("mid", part, way))
+            rs_send("four", part, way, q[pl.ds(2 * j + way, 1), lax.rem(z + 4, 8)], 2 * sign, ("mid", part, way))
+            rs_send("one", part, way, sums_for(1), sign, ("end", part))
         else:
+            arrived(("mid", part, way))
             value = sums_for(2) + rs_got("three", part, way)
             more = rs_got("four", part, way)
             parts = [value[:1] + more, value[1:]] if way == 0 else [value[:1], value[1:] + more]
-            rs_send("two", part, way, jnp.concatenate(parts, axis=0), 2 * sign)
+            rs_send("two", part, way, jnp.concatenate(parts, axis=0), 2 * sign, ("end", part))
 
     def rsend(part):
+        arrived(("end", part))
         value = q[pl.ds(2 * halves[part], 2), z]
         for way in (0, 1):
             value = value + rs_got("one", part, way) + rs_got("two", part, way)
         q[pl.ds(2 * halves[part], 2), z] = value
 
     def rsline():
-        sent["line"] = []
         for k in (1, 2, 3):
             line_out[k - 1] = q[flip(yl, k), z].astype(BF16)
-            sent["line"].append(copy(line_out.at[k - 1], line_in.at[k - 1], near_y[k - 1]))
+            copy(line_out.at[k - 1], line_in.at[k - 1], near_y[k - 1], "line")
 
     def igrad():
-        arrived(*sent["line"])
+        arrived("line")
         igrad_ref[...] = (
             q[yl, z] + line_in[0].astype(F32) + line_in[1].astype(F32) + line_in[2].astype(F32)
         ).astype(BF16)
@@ -297,25 +275,23 @@
             return carry
 
         lax.fori_loop(0, 3, body, 0)
-        sent["x", part] = [
-            copy(x_out.at[part, there, c], x_in.at[part, i], d)
-            for i, ((there, c), d) in enumerate(zip(row_places, near_row))
-        ]
+        for i, ((there, c), d) in enumerate(zip(row_places, near_row)):
+            copy(x_out.at[part, there, c], x_in.at[part, i], d, ("x", part))
 
     def fsum(part):
-        arrived(*sent["x", part])
+        arrived(("x", part))
         value = p[part, x, core]
         for i in range(7):
             value = value + x_in[part, i].astype(F32)
         if part == 0:
             y_out[...] = value.astype(BF16)
-            sent["y"] = copy(y_out, y_in, far_y)
+            copy(y_out, y_in, far_y, "y")
         else:
             sums[...] = value
 
     def hid():
         loaded(5)
-        arrived(sent["y"])
+        arrived("y")
         hidden_ref[...] = gelu_tanh(sums[...] + y_in[...].astype(F32) + bias[...]).astype(BF16)
 
     def bg():
@@ -347,8 +323,7 @@
                 gathers[what].step(*at)
         else:
             single[what](*at)
-    for c in started:
-        c.wait_send()
+    copies.finish(near_z[0])
 
 
 def local(tokens_fwd, tokens_bwd, weight, bias, preact, upstream):
@@ -388,9 +363,10 @@
             pltpu.VMEM((3, 16, 768), BF16),
             pltpu.VMEM((3, 16, 768), BF16),
             pltpu.VMEM((32, 768), F32),
+            pltpu.VMEM((SENT_ROWS, 768), BF16),
             pltpu.SemaphoreType.DMA((N_LOCAL,)),
-            pltpu.SemaphoreType.DMA((N_REMOTE,)),
-            pltpu.SemaphoreType.DMA((N_REMOTE,)),
+            pltpu.SemaphoreType.DMA,
+            pltpu.SemaphoreType.DMA((N_GROUPS,)),
         ],
         compiler_params=pltpu.CompilerParams(
             collective_id=0, has_side_effects=True, vmem_limit_bytes=48 * 2**20

time: 51 us -> 49.1 us (0.963)
  Pallas kernels: 46.8 us -> 44.9 us
    pallas_call x1, Pallas kernels: 46.8 us -> 44.9 us  [local(): pl.pallas_call(kernel, out_shape=shapes, in_specs=[hbm] * 6, out_specs=[v...]
where the time goes in v4:
time: 49.1 us; the launch traced here: 48.8 us
  Pallas kernels  44.9 us (91%)
  local copies, waits for them, and re-layouts  3.23 us (7%)
  between operations  0.64 us (1%)
    pallas_call x1, Pallas kernels, local(): pl.pallas_call(kernel, out_shape=shapes, in_specs=[hbm] * 6, out_specs=[v...  44.9 us
    unnamed x4, local copies, waits for them, and re-layouts  3.23 us

profile of v4, /device:TPU:6, one launch (start us, length us, event | category | flops | bytes accessed | tf_op | source)
XLA Modules:
  0.0 48.8 jit_solution(701977724178097209)
XLA Ops:
  0.6 44.9 %feed_forward.1 = (bf16[32,768]{1,0:T(8,128)(2,1)S(1)}, bf16[16,768]{1,0:T(8,128)(2,1)S(1)}, f32[768,768]{1,0:T(8,128)S(1)}, f32[768]{0:T(1024)S(1)}) custom-call(bf16[16,768]{1,0:T(8,128)(2,1)} %fwd_hbm.1, bf16[16,768]{1,0:T(8,128)(2,1)} %bwd_hbm.1, bf16[768,768]{1,0:T(8,128)(2,1)} %w_hbm.1, f32[768]{0:T(1024)} %bias_hbm.1, bf16[32,768]{1,0:T(8,128)(2,1)} %pre_hbm.1, ...), custom_call_target="tpu_custom_call" | custom-call | flops 1811939328 | bytes 8388608 | tf_op jit(solution)/shard_map/feed_forward/pallas_call | solution.py:342
  45.5 0.6 %copy.14 = bf16[32,768]{1,0:T(8,128)(2,1)} copy(bf16[32,768]{1,0:T(8,128)(2,1)S(1)} %get-tuple-element.8) | data formatting | bytes 98304
  46.2 0.6 %copy.15 = bf16[16,768]{1,0:T(8,128)(2,1)} copy(bf16[16,768]{1,0:T(8,128)(2,1)S(1)} %get-tuple-element.9) | data formatting | bytes 49152
  46.8 1.4 %copy.16 = f32[768,768]{1,0:T(8,128)} copy(f32[768,768]{1,0:T(8,128)S(1)} %get-tuple-element.10) | data formatting | bytes 4718592
  48.2 0.6 %copy.17 = f32[768]{0:T(1024)} copy(f32[768]{0:T(1024)S(1)} %get-tuple-element.11) | data formatting | bytes 6144

commit v5 on v4

--- a/solution.py
+++ b/solution.py
@@ -326,6 +326,15 @@
     copies.finish(near_z[0])
 
 
+def finish(*refs):
+    sem = refs[-1]
+    moves = [pltpu.make_async_copy(refs[i], refs[4 + i], sem.at[i]) for i in range(4)]
+    for c in moves:
+        c.start()
+    for c in moves:
+        c.wait()
+
+
 def local(tokens_fwd, tokens_bwd, weight, bias, preact, upstream):
     hbm = pl.BlockSpec(memory_space=pltpu.HBM)
     vmem = pl.BlockSpec(memory_space=pltpu.VMEM)
@@ -339,7 +348,7 @@
         pltpu.with_memory_space_constraint(a, pltpu.HBM)
         for a in (tokens_fwd, tokens_bwd, weight, bias, preact, upstream)
     ]
-    return pl.pallas_call(
+    results = pl.pallas_call(
         kernel,
         out_shape=shapes,
         in_specs=[hbm] * 6,
@@ -374,6 +383,15 @@
         cost_estimate=pl.CostEstimate(flops=3 * 2 * 512 * 768 * 768, bytes_accessed=8 * 2**20, transcendentals=50000),
         name="feed_forward",
     )(tokens_fwd, tokens_bwd, weight, bias, preact, upstream)
+    return pl.pallas_call(
+        finish,
+        out_shape=tuple(jax.ShapeDtypeStruct(r.shape, r.dtype) for r in results),
+        in_specs=[pl.BlockSpec(memory_space=pltpu.VMEM)] * 4,
+        out_specs=[pl.BlockSpec(memory_space=pl.ANY)] * 4,
+        scratch_shapes=[pltpu.SemaphoreType.DMA((4,))],
+        compiler_params=pltpu.CompilerParams(vmem_limit_bytes=1 << 20),
+        name="write_out",
+    )(*results)
 
 def solution(mesh):
     return jax.shard_map(

time: 49.1 us -> 47.4 us (0.965)
  local copies, waits for them, and re-layouts: 3.23 us -> 0 us
  Pallas kernels: 44.9 us -> 46.4 us
    unnamed x4 -> x0, local copies, waits for them, and re-layouts: 3.23 us -> none
    pallas_call x0 -> x1, Pallas kernels: none -> 1.47 us  [local(): pl.pallas_call(finish, out_shape=tuple((jax.ShapeDtypeStruct(r.shape, r.d...]
where the time goes in v5:
time: 47.4 us; the launch traced here: 47 us
  Pallas kernels  46.4 us (98%)
  between operations  0.64 us (1%)
    pallas_call x1, Pallas kernels, local(): pl.pallas_call(kernel, out_shape=shapes, in_specs=[hbm] * 6, out_specs=[v...  44.9 us
    pallas_call x1, Pallas kernels, local(): pl.pallas_call(finish, out_shape=tuple((jax.ShapeDtypeStruct(r.shape, r.d...  1.47 us

profile of v5, /device:TPU:6, one launch (start us, length us, event | category | flops | bytes accessed | tf_op | source)
XLA Modules:
  0.0 47.0 jit_solution(14417254767451432688)
XLA Ops:
  0.6 44.9 %feed_forward.1 = (bf16[32,768]{1,0:T(8,128)(2,1)S(1)}, bf16[16,768]{1,0:T(8,128)(2,1)S(1)}, f32[768,768]{1,0:T(8,128)S(1)}, f32[768]{0:T(1024)S(1)}) custom-call(bf16[16,768]{1,0:T(8,128)(2,1)} %fwd_hbm.1, bf16[16,768]{1,0:T(8,128)(2,1)} %bwd_hbm.1, bf16[768,768]{1,0:T(8,128)(2,1)} %w_hbm.1, f32[768]{0:T(1024)} %bias_hbm.1, bf16[32,768]{1,0:T(8,128)(2,1)} %pre_hbm.1, ...), custom_call_target="tpu_custom_call" | custom-call | flops 1811939328 | bytes 8388608 | tf_op jit(solution)/shard_map/feed_forward/pallas_call | solution.py:351
  45.5 1.5 %write_out.1 = (bf16[32,768]{1,0:T(8,128)(2,1)}, bf16[16,768]{1,0:T(8,128)(2,1)}, f32[768,768]{1,0:T(8,128)}, f32[768]{0:T(1024)}) custom-call(bf16[32,768]{1,0:T(8,128)(2,1)S(1)} %get-tuple-element.8.refs_0_, bf16[16,768]{1,0:T(8,128)(2,1)S(1)} %get-tuple-element.9.refs_1_, f32[768,768]{1,0:T(8,128)S(1)} %get-tuple-element.10.refs_2_, ...), custom_call_target="tpu_custom_call" | custom-call | tf_op jit(solution)/shard_map/write_out/pallas_call | solution.py:386

commit v6 on v5

--- a/solution.py
+++ b/solution.py
@@ -11,7 +11,7 @@
 cubic_term = 0.044715
 F32, BF16 = jnp.float32, jnp.bfloat16
 MESH = pl.DeviceIdType.MESH
-TILE = 256
+TILE = 384
 
 
 def gelu_tanh(values):
@@ -39,8 +39,8 @@
         self.extent, self.send, self.recv = extent, send, recv
         self.groups, self.waited, self.sent = {}, set(), 0
 
-    def start(self, src, dst, target, group):
-        rows = math.prod(dst.shape) // 768
+    def start(self, src, dst, target, group, again=False):
+        rows = 0 if again else math.prod(dst.shape) // 768
         number, before = self.groups.get(group, (len(self.groups), 0))
         self.groups[group] = (number, before + rows)
         self.sent += rows
@@ -68,11 +68,11 @@
 
 
 ORDER = (
-    ("b", 0, 0, 0), ("f", "line"), ("f", 0, 0, 0), ("far",), ("f", 0, 1, 0), ("spread", 0), ("b", 1, 0, 0),
-    ("b", 1, 0, 1), ("f", 0, 2, 0), ("f", 1, 1, 1), ("f", 1, 0, 1), ("spread", 1), ("b", "line"), ("f", 1, 1, 0),
-    ("f", 1, 0, 0), ("f", 1, 2, 1), ("f", 1, 2, 0), ("back", 0), ("rs", 0, 0, 1), ("rs", 0, 0, 0), ("back", 1),
-    ("rs", 0, 1, 0), ("rs", 0, 1, 1), ("fwd", 0), ("rs", 1, 0, 1), ("rs", 1, 0, 0), ("rs", 1, 1, 0), ("rs", 1, 1, 1),
-    ("fwd", 1), ("fsum", 0), ("rsend", 0), ("rsend", 1), ("rsline",), ("wg",), ("fsum", 1), ("bg",), ("hid",),
+    ("f", "line"), ("spread", 0), ("b", 0, 0, 0), ("f", 0, 0, 0), ("far",), ("f", 0, 1, 0), ("b", 1, 0, 0),
+    ("b", 1, 0, 1), ("f", 0, 2, 0), ("spread", 1), ("back", 0), ("rs", 0, 0, 1), ("b", "line"), ("f", 1, 0, 0),
+    ("f", 1, 2, 1), ("f", 1, 0, 1), ("f", 1, 1, 1), ("f", 1, 1, 0), ("f", 1, 2, 0), ("rs", 0, 0, 0), ("fwd", 0),
+    ("back", 1), ("rs", 0, 1, 0), ("rs", 0, 1, 1), ("fwd", 1), ("rs", 1, 0, 1), ("rs", 1, 0, 0), ("rs", 1, 1, 0),
+    ("rs", 1, 1, 1), ("fsum", 0), ("bg",), ("rsend", 0), ("rsend", 1), ("rsline",), ("wg",), ("fsum", 1), ("hid",),
     ("igrad",),
 )
 
@@ -80,7 +80,7 @@
 RS_SLOT = {"three": 0, "four": 2, "one": 3, "two": 5}
 RS_SIZE = {"three": 2, "four": 1, "one": 2, "two": 2}
 N_LOCAL = 6
-N_GROUPS = 26
+N_GROUPS = 28
 SENT_ROWS = 2448
 
 
@@ -150,7 +150,7 @@
 
         def line(self):
             if self.z_first:
-                arrived((self.name, "rest"))
+                arrived((self.name, 1), (self.name, "rest"))
                 loaded(4)
                 block = src = self.ref.at[yl]
             else:
@@ -173,7 +173,7 @@
                 for way in (0, 1):
                     copy(src, block, along_z[(2, -2)[way]], (self.name, 2, which, way))
                 for way in (0, 1):
-                    copy(src, block, along_z[(1, -1)[way]], (self.name, "rest"))
+                    copy(src, block, along_z[(1, -1)[way]], (self.name, 1))
                 return
             arrived((self.name, 2, which, way))
             sign = (1, -1)[way]
@@ -184,6 +184,9 @@
             block = self.block(which, source)
             copy(block, block, along_z[sign], (self.name, "rest"))
 
+        def near(self):
+            arrived((self.name, 1), *((self.name, 2, which, way) for which in (0, 1, 2) for way in (0, 1)))
+
         def finish(self):
             arrived((self.name, "line", 0) if self.z_first else (self.name, "rest"))
 
@@ -214,7 +217,7 @@
             ).reshape(2, 8, 16, TILE)
             return carry
 
-        lax.fori_loop(0, 3, body, 0)
+        lax.fori_loop(0, 2, body, 0)
 
     def rs_send(name, part, way, value, away, group):
         slots = pl.ds(RS_SLOT[name] + 7 * (2 * part + way), value.shape[0])
@@ -259,28 +262,42 @@
             q[yl, z] + line_in[0].astype(F32) + line_in[1].astype(F32) + line_in[2].astype(F32)
         ).astype(BF16)
 
-    f_halves = (1 - yh, yh)
-
-    def fwd(part):
-        gathers["f"].finish()
+    odd = lax.rem(z, 2)
+    near_pairs = (z // 2, lax.rem(z // 2 + 2 * odd + 3, 4))
+    far_pairs = (lax.rem(z // 2 + 2, 4), lax.rem(z // 2 + 5 - 2 * odd, 4))
+
+    def block_of(part, there, c):
+        return 2 * (1 - yh, yh)[part] + there // 2, 2 * lax.rem(there, 2) + c
+
+    def fwd(phase):
         loaded(0, 3)
-        j = f_halves[part]
-        rows = xf[pl.ds(2 * j, 2)].reshape(256, 768)
+        if phase == 0:
+            gathers["f"].near()
+        else:
+            gathers["f"].finish()
+        pairs = (near_pairs, far_pairs)[phase]
+        rows = jnp.concatenate([xf[:, pair // 2, lax.rem(pair, 2)].reshape(128, 768) for pair in pairs], axis=0)
 
         def body(n, carry):
             at = pl.ds(pl.multiple_of(n * TILE, TILE), TILE)
-            value = jnp.dot(rows, w[:, at], preferred_element_type=F32).reshape(4, 2, 32, TILE)
-            p[part, :, :, :, at] = value
-            x_out[part, :, :, :, at] = value.astype(BF16)
+            value = jnp.dot(rows, w[:, at], preferred_element_type=F32).reshape(2, 4, 32, TILE)
+            for i, pair in enumerate(pairs):
+                p[:, pair, :, at] = value[i]
+                x_out[:, pair, :, at] = value[i].astype(BF16)
             return carry
 
-        lax.fori_loop(0, 3, body, 0)
-        for i, ((there, c), d) in enumerate(zip(row_places, near_row)):
-            copy(x_out.at[part, there, c], x_in.at[part, i], d, ("x", part))
+        lax.fori_loop(0, 2, body, 0)
+        for part in (0, 1):
+            for i, ((there, c), d) in enumerate(zip(row_places, near_row)):
+                at = block_of(part, there, c)
+
+                @pl.when((at[1] == pairs[0]) | (at[1] == pairs[1]))
+                def _():
+                    copy(x_out.at[at], x_in.at[part, i], d, ("x", part), again=phase == 1)
 
     def fsum(part):
         arrived(("x", part))
-        value = p[part, x, core]
+        value = p[block_of(part, x, core)]
         for i in range(7):
             value = value + x_in[part, i].astype(F32)
         if part == 0:
@@ -309,7 +326,7 @@
             )
             return carry
 
-        lax.fori_loop(0, 3, body, 0)
+        lax.fori_loop(0, 2, body, 0)
 
     single = dict(
         far=far, spread=spread, back=back, rs=rs, rsend=rsend, rsline=rsline, igrad=igrad,
@@ -362,8 +379,8 @@
             pltpu.VMEM((768,), F32),
             pltpu.VMEM((32, 768), BF16),
             pltpu.VMEM((32, 768), BF16),
-            pltpu.VMEM((2, 4, 2, 32, 768), F32),
-            pltpu.VMEM((2, 4, 2, 32, 768), BF16),
+            pltpu.VMEM((4, 4, 32, 768), F32),
+            pltpu.VMEM((4, 4, 32, 768), BF16),
             pltpu.VMEM((2, 7, 32, 768), BF16),
             pltpu.VMEM((32, 768), BF16),
             pltpu.VMEM((32, 768), BF16),

time: 47.4 us -> 47.2 us (level)
  no operation moved by 1% of the time
where the time goes in v6:
time: 47.2 us; the launch traced here: 47 us
  Pallas kernels  46.4 us (98%)
  between operations  0.64 us (1%)
    pallas_call x1, Pallas kernels, local(): pl.pallas_call(kernel, out_shape=shapes, in_specs=[hbm] * 6, out_specs=[v...  44.9 us
    pallas_call x1, Pallas kernels, local(): pl.pallas_call(finish, out_shape=tuple((jax.ShapeDtypeStruct(r.shape, r.d...  1.47 us

profile of v6, /device:TPU:6, one launch (start us, length us, event | category | flops | bytes accessed | tf_op | source)
XLA Modules:
  0.0 47.0 jit_solution(17840473276368396097)
XLA Ops:
  0.6 44.9 %feed_forward.1 = (bf16[32,768]{1,0:T(8,128)(2,1)S(1)}, bf16[16,768]{1,0:T(8,128)(2,1)S(1)}, f32[768,768]{1,0:T(8,128)S(1)}, f32[768]{0:T(1024)S(1)}) custom-call(bf16[16,768]{1,0:T(8,128)(2,1)} %fwd_hbm.1, bf16[16,768]{1,0:T(8,128)(2,1)} %bwd_hbm.1, bf16[768,768]{1,0:T(8,128)(2,1)} %w_hbm.1, f32[768]{0:T(1024)} %bias_hbm.1, bf16[32,768]{1,0:T(8,128)(2,1)} %pre_hbm.1, ...), custom_call_target="tpu_custom_call" | custom-call | flops 1811939328 | bytes 8388608 | tf_op jit(solution)/shard_map/feed_forward/pallas_call | solution.py:368
  45.6 1.5 %write_out.1 = (bf16[32,768]{1,0:T(8,128)(2,1)}, bf16[16,768]{1,0:T(8,128)(2,1)}, f32[768,768]{1,0:T(8,128)}, f32[768]{0:T(1024)}) custom-call(bf16[32,768]{1,0:T(8,128)(2,1)S(1)} %get-tuple-element.8.refs_0_, bf16[16,768]{1,0:T(8,128)(2,1)S(1)} %get-tuple-element.9.refs_1_, f32[768,768]{1,0:T(8,128)S(1)} %get-tuple-element.10.refs_2_, ...), custom_call_target="tpu_custom_call" | custom-call | tf_op jit(solution)/shard_map/write_out/pallas_call | solution.py:403

commit v7 on v6

--- a/solution.py
+++ b/solution.py
@@ -68,12 +68,12 @@
 
 
 ORDER = (
-    ("f", "line"), ("spread", 0), ("b", 0, 0, 0), ("f", 0, 0, 0), ("far",), ("f", 0, 1, 0), ("b", 1, 0, 0),
-    ("b", 1, 0, 1), ("f", 0, 2, 0), ("spread", 1), ("back", 0), ("rs", 0, 0, 1), ("b", "line"), ("f", 1, 0, 0),
-    ("f", 1, 2, 1), ("f", 1, 0, 1), ("f", 1, 1, 1), ("f", 1, 1, 0), ("f", 1, 2, 0), ("rs", 0, 0, 0), ("fwd", 0),
-    ("back", 1), ("rs", 0, 1, 0), ("rs", 0, 1, 1), ("fwd", 1), ("rs", 1, 0, 1), ("rs", 1, 0, 0), ("rs", 1, 1, 0),
-    ("rs", 1, 1, 1), ("fsum", 0), ("bg",), ("rsend", 0), ("rsend", 1), ("rsline",), ("wg",), ("fsum", 1), ("hid",),
-    ("igrad",),
+    ("f", "line"), ("f", 0, 0, 0), ("grad",), ("far",), ("spread", 0), ("b", 0, 0, 0), ("f", 0, 1, 0),
+    ("b", 1, 0, 0), ("b", 1, 0, 1), ("f", 0, 2, 0), ("spread", 1), ("back", 0), ("rs", 0, 0, 1), ("b", "line"),
+    ("f", 1, 0, 0), ("f", 1, 2, 1), ("f", 1, 0, 1), ("f", 1, 1, 1), ("f", 1, 1, 0), ("f", 1, 2, 0), ("rs", 0, 0, 0),
+    ("fwd", 0), ("back", 1), ("rs", 0, 1, 0), ("rs", 0, 1, 1), ("fwd", 1), ("rs", 1, 0, 1), ("rs", 1, 0, 0),
+    ("rs", 1, 1, 0), ("rs", 1, 1, 1), ("fsum", 0), ("bg",), ("rsend", 0), ("rsend", 1), ("rsline",), ("wg",),
+    ("fsum", 1), ("hid",), ("igrad",),
 )
 
 
@@ -131,12 +131,9 @@
         pl.semaphore_signal(barrier, inc=1, device_id=d, device_id_type=MESH)
     for c in loads:
         c.start()
-    loads[1].wait()
-    loads[2].wait()
-    g[yh, x, core] = (up[...].astype(F32) * gelu_slope(pre[...].astype(F32))).astype(BF16)
     pl.semaphore_wait(barrier, len(partners))
 
-    waited = {1, 2}
+    waited = set()
 
     def loaded(*which):
         for i in which:
@@ -192,6 +189,10 @@
 
     gathers = {"f": Gather("f", fwd_hbm, xf, False), "b": Gather("b", bwd_hbm, xb, True)}
 
+    def grad():
+        loaded(1, 2)
+        g[yh, x, core] = (up[...].astype(F32) * gelu_slope(pre[...].astype(F32))).astype(BF16)
+
     def far():
         copy(g.at[yh, x, core], g.at[yh, x, core], far_y, "far")
 
@@ -329,7 +330,7 @@
         lax.fori_loop(0, 2, body, 0)
 
     single = dict(
-        far=far, spread=spread, back=back, rs=rs, rsend=rsend, rsline=rsline, igrad=igrad,
+        grad=grad, far=far, spread=spread, back=back, rs=rs, rsend=rsend, rsline=rsline, igrad=igrad,
         fwd=fwd, fsum=fsum, hid=hid, bg=bg, wg=wg,
     )
     for what, *at in ORDER:

time: 47.2 us -> 48.4 us (1.025)
  the two profiles are of different devices: /device:TPU:6 before, /device:TPU:1 now
where the time goes in v7:
time: 48.4 us; the launch traced here: 48.3 us
  Pallas kernels  47.7 us (99%)
  between operations  0.64 us (1%)
    pallas_call x1, Pallas kernels, local(): pl.pallas_call(kernel, out_shape=shapes, in_specs=[hbm] * 6, out_specs=[v...  46.2 us
    pallas_call x1, Pallas kernels, local(): pl.pallas_call(finish, out_shape=tuple((jax.ShapeDtypeStruct(r.shape, r.d...  1.47 us

profile of v7, /device:TPU:1, one launch (start us, length us, event | category | flops | bytes accessed | tf_op | source)
XLA Modules:
  0.0 48.3 jit_solution(12349560319457113348)
XLA Ops:
  0.6 46.2 %feed_forward.1 = (bf16[32,768]{1,0:T(8,128)(2,1)S(1)}, bf16[16,768]{1,0:T(8,128)(2,1)S(1)}, f32[768,768]{1,0:T(8,128)S(1)}, f32[768]{0:T(1024)S(1)}) custom-call(bf16[16,768]{1,0:T(8,128)(2,1)} %fwd_hbm.1, bf16[16,768]{1,0:T(8,128)(2,1)} %bwd_hbm.1, bf16[768,768]{1,0:T(8,128)(2,1)} %w_hbm.1, f32[768]{0:T(1024)} %bias_hbm.1, bf16[32,768]{1,0:T(8,128)(2,1)} %pre_hbm.1, ...), custom_call_target="tpu_custom_call" | custom-call | flops 1811939328 | bytes 8388608 | tf_op jit(solution)/shard_map/feed_forward/pallas_call | solution.py:369
  46.8 1.5 %write_out.1 = (bf16[32,768]{1,0:T(8,128)(2,1)}, bf16[16,768]{1,0:T(8,128)(2,1)}, f32[768,768]{1,0:T(8,128)}, f32[768]{0:T(1024)}) custom-call(bf16[32,768]{1,0:T(8,128)(2,1)S(1)} %get-tuple-element.8.refs_0_, bf16[16,768]{1,0:T(8,128)(2,1)S(1)} %get-tuple-element.9.refs_1_, f32[768,768]{1,0:T(8,128)S(1)} %get-tuple-element.10.refs_2_, ...), custom_call_target="tpu_custom_call" | custom-call | tf_op jit(solution)/shard_map/write_out/pallas_call | solution.py:404
